TPU v7x, 32 devices: a whole 2x2x4 slice. The times are simulated.
32 devices in a mesh: ctx: 16 (over z, y, core), tp: 2 (over x).
Axes of the slice: x: 2, y: 2, z: 4, core: 2. Of those that a mesh axis runs over, the one named last changes fastest.
Arguments:
- inputs: bfloat16 [3072, 2048], P('ctx'), may hold values from -8 to 8
- norm1_gain: float32 [2048], replicated, may hold values from 0.1 to 1.9
- query_weight: bfloat16 [2048, 2048], P('ctx', 'tp'), may hold values from -0.125 to 0.125
- key_weight: bfloat16 [2048, 512], P('ctx', 'tp'), may hold values from -0.125 to 0.125
- value_weight: bfloat16 [2048, 512], P('ctx', 'tp'), may hold values from -0.125 to 0.125
- query_gain: float32 [64], replicated, may hold values from 0.1 to 1.9
- key_gain: float32 [64], replicated, may hold values from 0.1 to 1.9
- out_weight: bfloat16 [2048, 2048], P('tp', 'ctx'), may hold values from -3 to 3
- norm2_gain: float32 [2048], replicated, may hold values from 0.1 to 1.9
- gate_weight: bfloat16 [2048, 8192], P('ctx', 'tp'), may hold values from -0.125 to 0.125
- up_weight: bfloat16 [2048, 8192], P('ctx', 'tp'), may hold values from -0.125 to 0.125
- down_weight: bfloat16 [8192, 2048], P('tp', 'ctx'), may hold values from -0.0625 to 0.0625
- doc_starts: int32 [4], replicated, may hold values from 0 to 3071, as said below
- cotangent: bfloat16 [3072, 2048], P('ctx'), may hold values from -8 to 8
Outputs:
- output: bfloat16 [3072, 2048], P('ctx')
- input_grad: bfloat16 [3072, 2048], P('ctx')
- norm1_grad: float32 [2048], replicated
- query_grad: float32 [2048, 2048], P('ctx', 'tp')
- key_grad: float32 [2048, 512], P('ctx', 'tp')
- value_grad: float32 [2048, 512], P('ctx', 'tp')
- query_gain_grad: float32 [64], replicated
- key_gain_grad: float32 [64], replicated
- out_grad: float32 [2048, 2048], P('tp', 'ctx')
- norm2_grad: float32 [2048], replicated
- gate_grad: float32 [2048, 8192], P('ctx', 'tp')
- up_grad: float32 [2048, 8192], P('ctx', 'tp')
- down_grad: float32 [8192, 2048], P('tp', 'ctx')
Inputs may be any that keep to these rules, and one draw needn't show every extreme that they name: `doc_starts`: strictly increasing; the first entry is 0, the second lies in 1 .. 191, the third in 2881 .. 2975 and the fourth in 2976 .. 3071.
All inputs are finite; a program needn't handle non-finite values.
Results may differ from a plain program's by a relative error of at most 0.018.
Values may be sent and summed in bfloat16 or wider, within the bound.
No kernel may reach another device: no remote copies, remote signals or barrier semaphores. Data moves between devices by JAX's collectives and lax.ppermute only.
A program may use at most 248 MiB of HBM per device.

v0:
```python
import jax
import jax.numpy as jnp
from jax import lax
from jax.sharding import PartitionSpec as P

epsilon = 1e-05
rope_base = 1000000.0
neg_large = -1e30


def norm_rows(values, gain):
    inverse = lax.rsqrt(jnp.mean(values * values, axis=-1, keepdims=True) + epsilon)
    unit_rows = values * inverse
    return (unit_rows * gain, unit_rows, inverse)


def norm_back(grad_out, gain, unit_rows, inverse):
    scaled = grad_out * gain
    inner_mean = jnp.mean(scaled * unit_rows, axis=-1, keepdims=True)
    return inverse * (scaled - unit_rows * inner_mean)


def angles(positions, head_width):
    half_width = head_width // 2
    ladder = jnp.arange(half_width, dtype=jnp.float32)
    freq_table = 1.0 / rope_base ** (ladder * 2.0 / head_width)
    turned = positions.astype(jnp.float32)[:, None] * freq_table[None, :]
    return (jnp.cos(turned)[:, None, :], jnp.sin(turned)[:, None, :])


def rotate(values, cosine, sine_table):
    half_width = values.shape[-1] // 2
    first_half = values[..., :half_width]
    second_half = values[..., half_width:]
    return jnp.concatenate(
        [
            first_half * cosine - second_half * sine_table,
            second_half * cosine + first_half * sine_table,
        ],
        axis=-1,
    )


def document_info(positions, starts):
    inside = starts[None, :] <= positions[:, None]
    ident = jnp.sum(inside.astype(jnp.int32), axis=1) - 1
    begin = jnp.max(jnp.where(inside, starts[None, :], 0), axis=1)
    return (ident, positions - begin)


def times_transposed(left_side, right_side):
    return lax.dot_general(
        left_side, right_side, (((1,), (1,)), ((), ())), preferred_element_type=jnp.float32
    )


def transposed_times(left_side, right_side):
    return lax.dot_general(
        left_side, right_side, (((0,), (0,)), ((), ())), preferred_element_type=jnp.float32
    )


def split_count(row_count):
    pieces = 1
    while row_count % pieces != 0 or row_count // pieces > 512:
        pieces += 1
    return pieces


def blockwise(step, state, members):
    row_count = members[0].shape[0]
    pieces = split_count(row_count)
    size_each = row_count // pieces
    stacked = tuple((member.reshape((pieces, size_each) + member.shape[1:]) for member in members))
    firsts = size_each * jnp.arange(pieces, dtype=jnp.int32)

    def advance(carried, element):
        return (step(carried, element[0], element[1]), None)

    final_state, unused = lax.scan(advance, state, (stacked, firsts))
    return final_state


def shards(
    inputs,
    norm1_gain,
    query_weight,
    key_weight,
    value_weight,
    query_gain,
    key_gain,
    out_weight,
    norm2_gain,
    gate_weight,
    up_weight,
    down_weight,
    doc_starts,
    cotangent,
):
    context_place = lax.axis_index("ctx")
    tok_rows = inputs.shape[0]
    head_width = query_gain.shape[0]
    query_columns = query_weight.shape[1]
    key_columns = key_weight.shape[1]
    hidden_columns = gate_weight.shape[1]
    query_heads = query_columns // head_width
    key_heads = key_columns // head_width
    heads_per_group = query_heads // key_heads
    score_scale = head_width ** (-0.5)
    own_first = context_place * tok_rows
    own_positions = own_first + jnp.arange(tok_rows, dtype=jnp.int32)
    own_document, own_offset = document_info(own_positions, doc_starts)
    cosine, sine_table = angles(own_offset, head_width)

    def score_block(query_block, key_block, query_first, key_first):
        raw_scores = (
            jnp.einsum("tkgd,jkd->kgtj", query_block, key_block, preferred_element_type=jnp.float32)
            * score_scale
        )
        query_place = query_first + jnp.arange(query_block.shape[0], dtype=jnp.int32)
        key_place = key_first + jnp.arange(key_block.shape[0], dtype=jnp.int32)
        query_doc = document_info(query_place, doc_starts)[0]
        key_doc = document_info(key_place, doc_starts)[0]
        allow = (key_place[None, :] <= query_place[:, None]) & (
            key_doc[None, :] == query_doc[:, None]
        )
        allow = allow[None, None]
        return (jnp.where(allow, raw_scores, neg_large), allow)

    united_rows = jnp.concatenate([query_weight, key_weight, value_weight], axis=1)
    paired = jnp.stack([gate_weight, up_weight])
    full_rows, full_pair, full_out, full_down = (
        lax.all_gather(united_rows, "ctx", axis=0, tiled=True),
        lax.all_gather(paired, "ctx", axis=1, tiled=True),
        lax.all_gather(out_weight, "ctx", axis=1, tiled=True),
        lax.all_gather(down_weight, "ctx", axis=1, tiled=True),
    )
    in_float = inputs.astype(jnp.float32)
    first_normalized, unit_one, scale_one = norm_rows(in_float, norm1_gain)
    first_low = first_normalized.astype(jnp.bfloat16)
    projected = jnp.dot(first_low, full_rows, preferred_element_type=jnp.float32)
    query_raw = projected[:, :query_columns].reshape(tok_rows, query_heads, head_width)
    key_raw = projected[:, query_columns : query_columns + key_columns].reshape(
        tok_rows, key_heads, head_width
    )
    value_low = projected[:, query_columns + key_columns :].astype(jnp.bfloat16)
    query_normed, query_unit, query_scale = norm_rows(query_raw, query_gain)
    key_normed, key_unit, key_scale = norm_rows(key_raw, key_gain)
    query_low = (
        rotate(query_normed, cosine, sine_table)
        .astype(jnp.bfloat16)
        .reshape(tok_rows, key_heads, heads_per_group, head_width)
    )
    key_low = (
        rotate(key_normed, cosine, sine_table).astype(jnp.bfloat16).reshape(tok_rows, key_columns)
    )
    packed = jnp.concatenate([key_low, value_low], axis=1)

    def maxima_step(state, block_members, key_first):
        row_top, row_total = state
        block_keys = block_members[0].reshape(-1, key_heads, head_width)
        masked, allow = score_block(query_low, block_keys, own_first, key_first)
        new_top = jnp.maximum(row_top, jnp.max(masked, axis=-1))
        row_total = row_total * jnp.exp(row_top - new_top) + jnp.sum(
            jnp.where(allow, jnp.exp(masked - new_top[..., None]), 0.0), axis=-1
        )
        return (new_top, row_total)

    stat_shape = (key_heads, heads_per_group, tok_rows)
    row_top, row_total = blockwise(
        maxima_step,
        (jnp.full(stat_shape, neg_large, jnp.float32), jnp.zeros(stat_shape, jnp.float32)),
        (lax.all_gather(key_low, "ctx", axis=0, tiled=True),),
    )
    row_lse = row_top + jnp.log(row_total)

    def output_step(accum, block_members, key_first):
        block_keys = block_members[0][:, :key_columns].reshape(-1, key_heads, head_width)
        block_values = block_members[0][:, key_columns:].reshape(-1, key_heads, head_width)
        masked, allow = score_block(query_low, block_keys, own_first, key_first)
        weights = jnp.where(allow, jnp.exp(masked - row_lse[..., None]), 0.0).astype(jnp.bfloat16)
        return accum + jnp.einsum(
            "kgtj,jkd->tkgd", weights, block_values, preferred_element_type=jnp.float32
        )

    head_shape = (tok_rows, key_heads, heads_per_group, head_width)
    mixed_float = blockwise(
        output_step,
        jnp.zeros(head_shape, jnp.float32),
        (lax.all_gather(packed, "ctx", axis=0, tiled=True),),
    )
    mixed_low = mixed_float.reshape(tok_rows, query_columns).astype(jnp.bfloat16)
    attended = lax.psum(
        jnp.dot(mixed_low, full_out, preferred_element_type=jnp.float32).astype(jnp.bfloat16), "tp"
    ).astype(jnp.float32)
    middle = in_float + attended
    normed_two, unit_two, scale_two = norm_rows(middle, norm2_gain)
    second_low = normed_two.astype(jnp.bfloat16)
    gate_vals = jnp.dot(second_low, full_pair[0], preferred_element_type=jnp.float32)
    up_vals = jnp.dot(second_low, full_pair[1], preferred_element_type=jnp.float32)
    gate_sigmoid = jax.nn.sigmoid(gate_vals)
    hidden_low = (gate_vals * gate_sigmoid * up_vals).astype(jnp.bfloat16)
    branch_sum = lax.psum(
        jnp.dot(hidden_low, full_down, preferred_element_type=jnp.float32).astype(jnp.bfloat16),
        "tp",
    ).astype(jnp.float32)
    output = (middle + branch_sum).astype(jnp.bfloat16)
    back_rows, back_pair, back_out, back_down = (
        lax.all_gather(united_rows, "ctx", axis=0, tiled=True),
        lax.all_gather(paired, "ctx", axis=1, tiled=True),
        lax.all_gather(out_weight, "ctx", axis=1, tiled=True),
        lax.all_gather(down_weight, "ctx", axis=1, tiled=True),
    )
    grad_hidden = times_transposed(cotangent, back_down)
    grad_gate = (
        grad_hidden * up_vals * gate_sigmoid * (1.0 + gate_vals * (1.0 - gate_sigmoid))
    ).astype(jnp.bfloat16)
    grad_up = (grad_hidden * gate_vals * gate_sigmoid).astype(jnp.bfloat16)
    grad_second_part = times_transposed(grad_gate, back_pair[0]) + times_transposed(
        grad_up, back_pair[1]
    )
    gain_two_term = jnp.sum(grad_second_part * unit_two, axis=0)
    grad_second = lax.psum(grad_second_part.astype(jnp.bfloat16), "tp").astype(jnp.float32)
    grad_middle = cotangent.astype(jnp.float32) + norm_back(
        grad_second, norm2_gain, unit_two, scale_two
    )
    grad_attended = grad_middle.astype(jnp.bfloat16)
    grad_mixed = times_transposed(grad_attended, back_out).astype(jnp.bfloat16)
    grad_heads = grad_mixed.reshape(head_shape)
    row_delta = jnp.transpose(
        jnp.sum(grad_heads.astype(jnp.float32) * mixed_float, axis=-1), (1, 2, 0)
    )
    all_keys = lax.all_gather(packed, "ctx", axis=0, tiled=True)
    total_rows = all_keys.shape[0]
    key_pieces = split_count(total_rows)
    key_size = total_rows // key_pieces
    stacked_keys = all_keys.reshape(key_pieces, key_size, 2 * key_columns)
    key_firsts = key_size * jnp.arange(key_pieces, dtype=jnp.int32)

    def backward_step(accum, element):
        block_rows, key_first = element
        block_keys = block_rows[:, :key_columns].reshape(-1, key_heads, head_width)
        block_values = block_rows[:, key_columns:].reshape(-1, key_heads, head_width)
        masked, allow = score_block(query_low, block_keys, own_first, key_first)
        probs = jnp.where(allow, jnp.exp(masked - row_lse[..., None]), 0.0)
        grad_probs = jnp.einsum(
            "tkgd,jkd->kgtj", grad_heads, block_values, preferred_element_type=jnp.float32
        )
        grad_scores = (probs * (grad_probs - row_delta[..., None])).astype(jnp.bfloat16)
        accum = (
            accum
            + jnp.einsum(
                "kgtj,jkd->tkgd", grad_scores, block_keys, preferred_element_type=jnp.float32
            )
            * score_scale
        )
        key_piece = (
            jnp.einsum("kgtj,tkgd->jkd", grad_scores, query_low, preferred_element_type=jnp.float32)
            * score_scale
        )
        value_piece = jnp.einsum(
            "kgtj,tkgd->jkd",
            probs.astype(jnp.bfloat16),
            grad_heads,
            preferred_element_type=jnp.float32,
        )
        return (
            accum,
            jnp.concatenate(
                [key_piece.reshape(-1, key_columns), value_piece.reshape(-1, key_columns)], axis=1
            ),
        )

    grad_query, key_terms = lax.scan(
        backward_step, jnp.zeros(head_shape, jnp.float32), (stacked_keys, key_firsts)
    )
    key_terms = key_terms.reshape(total_rows, 2 * key_columns)
    key_value_grads = lax.psum_scatter(key_terms, "ctx", scatter_dimension=0, tiled=True)
    key_shape = (tok_rows, key_heads, head_width)
    grad_key_rot = key_value_grads[:, :key_columns].reshape(key_shape)
    grad_value = key_value_grads[:, key_columns:]
    grad_query_normed = rotate(
        grad_query.reshape(tok_rows, query_heads, head_width), cosine, -sine_table
    )
    grad_query_raw = norm_back(grad_query_normed, query_gain, query_unit, query_scale)
    query_gain_term = jnp.sum(grad_query_normed * query_unit, axis=(0, 1))
    grad_key_normed = rotate(grad_key_rot, cosine, -sine_table)
    grad_key_raw = norm_back(grad_key_normed, key_gain, key_unit, key_scale)
    key_gain_term = jnp.sum(grad_key_normed * key_unit, axis=(0, 1))
    grad_proj = jnp.concatenate(
        [
            grad_query_raw.reshape(tok_rows, query_columns),
            grad_key_raw.reshape(tok_rows, key_columns),
            grad_value,
        ],
        axis=1,
    ).astype(jnp.bfloat16)
    grad_first_part = times_transposed(grad_proj, back_rows)
    gain_one_term = jnp.sum(grad_first_part * unit_one, axis=0)
    grad_first = lax.psum(grad_first_part.astype(jnp.bfloat16), "tp").astype(jnp.float32)
    input_grad = (grad_middle + norm_back(grad_first, norm1_gain, unit_one, scale_one)).astype(
        jnp.bfloat16
    )
    united_width = query_columns + 2 * key_columns
    left_one = first_low
    left_two = second_low
    row_grads = lax.psum_scatter(
        jnp.concatenate(
            [
                transposed_times(left_one, grad_proj),
                transposed_times(left_two, grad_gate),
                transposed_times(left_two, grad_up),
            ],
            axis=1,
        ),
        "ctx",
        scatter_dimension=0,
        tiled=True,
    )
    left_one = grad_attended
    left_two = cotangent
    column_grads = lax.psum_scatter(
        jnp.concatenate(
            [transposed_times(left_one, mixed_low), transposed_times(left_two, hidden_low)], axis=1
        ),
        "ctx",
        scatter_dimension=0,
        tiled=True,
    )
    norm1_grad, query_gain_grad, key_gain_grad, norm2_grad = lax.psum(
        (gain_one_term, query_gain_term, key_gain_term, gain_two_term), ("ctx", "tp")
    )
    query_grad = row_grads[:, :query_columns]
    key_grad = row_grads[:, query_columns : query_columns + key_columns]
    value_grad = row_grads[:, query_columns + key_columns : united_width]
    gate_grad = row_grads[:, united_width : united_width + hidden_columns]
    up_grad = row_grads[:, united_width + hidden_columns :]
    out_grad = jnp.transpose(column_grads[:, :query_columns])
    down_grad = jnp.transpose(column_grads[:, query_columns:])
    return (
        output,
        input_grad,
        norm1_grad,
        query_grad,
        key_grad,
        value_grad,
        query_gain_grad,
        key_gain_grad,
        out_grad,
        norm2_grad,
        gate_grad,
        up_grad,
        down_grad,
    )


def solution(mesh):
    placed = (
        P("ctx", None),
        P(),
        P("ctx", "tp"),
        P("ctx", "tp"),
        P("ctx", "tp"),
        P(),
        P(),
        P("tp", "ctx"),
        P(),
        P("ctx", "tp"),
        P("ctx", "tp"),
        P("tp", "ctx"),
        P(),
        P("ctx", None),
    )
    return jax.shard_map(
        shards,
        mesh=mesh,
        in_specs=placed,
        out_specs=(
            P("ctx", None),
            P("ctx", None),
            P(),
            P("ctx", "tp"),
            P("ctx", "tp"),
            P("ctx", "tp"),
            P(),
            P(),
            P("tp", "ctx"),
            P(),
            P("ctx", "tp"),
            P("ctx", "tp"),
            P("tp", "ctx"),
        ),
        check_vma=False,
    )
```

profile of v0, /device:TPU:0, one launch (start us, length us, event | category | flops | bytes accessed | tf_op | source)
XLA Modules:
  0.0 2044.7 jit_solution(3483770965700687115)
XLA Ops:
  12.1 63.4 %all-gather.7.cloned.1.call-done = bf16[2048,1536]{1,0:T(8,128)(2,1)} async-done(((bf16[128,1536]{1,0:T(8,128)(2,1)}), bf16[2048,1536]{1,0:T(8,128)(2,1)}) %all-gather.7.cloned.1.call-update) | async-done | bytes 6291472 | tf_op jit(solution)/shard_map/all_gather | solution.py:133
  75.5 4.5 fusion.59
  87.7 32.5 %all-gather.11.cloned.1.call-done = bf16[3072,256]{1,0:T(8,128)(2,1)} async-done(((bf16[192,256]{1,0:T(8,128)(2,1)}), bf16[3072,256]{1,0:T(8,128)(2,1)}) %all-gather.11.cloned.1.call-update) | async-done | bytes 1572880 | tf_op jit(solution)/shard_map/all_gather | solution.py:173
  120.3 37.1 %while.46 = (s32[]{:T(128)}, f32[4,4,192]{2,1,0:T(4,128)S(1)}, f32[4,4,192]{2,1,0:T(4,128)S(1)}, s32[6]{0:T(128)S(1)}, s32[]{:T(128)}, /*index=5*/s32[4]{0:T(128...) while((s32[]{:T(128)}, f32[4,4,192]{2,1,0:T(4,128)S(1)}, ...), condition=%wide.region_9.10_spmd.clone, body=%wide.region_4.9_spmd.clone.sunk | while | flops 214228928 | bytes 14761392 | solution.py:80
  157.4 9.8 all-gather.9.cloned.1.call-done
  167.2 4.7 copy.107
  172.0 34.6 %while.47 = (s32[]{:T(128)}, f32[192,4,4,64]{0,3,2,1:T(8,128)S(1)}, bf16[6,512,512]{1,2,0:T(8,128)(2,1)}, s32[6]{0:T(128)S(1)}, s32[]{:T(128)}, /*index=5*/s32[4...) while((s32[]{:T(128)}, f32[192,4,4,64]{0,3,2,1:T(8,128)S(1)}, ...), condition=%wide.region_13.14_spmd.clone, body=%wide.region_10.13_spmd.clone.sunk | while | flops 411214784 | bytes 4816303 | solution.py:80
  206.6 14.7 all-gather.13.cloned.1.call-done
  229.6 28.6 %all-reduce.6.cloned.1.call-done = bf16[192,2048]{1,0:T(8,128)(2,1)} async-done(((bf16[192,2048]{1,0:T(8,128)(2,1)}), bf16[192,2048]{1,0:T(8,128)(2,1)}) %all-reduce.6.cloned.1.call-update) | async-done | bytes 786448 | tf_op jit(solution)/shard_map/psum | solution.py:193
  261.2 167.2 %all-gather.15.cloned.1.call-done = bf16[2,2048,4096]{2,1,0:T(8,128)(2,1)} async-done(((bf16[2,128,4096]{2,1,0:T(8,128)(2,1)}), bf16[2,2048,4096]{2,1,0:T(8,128)(2,1)}) %all-gather.15.cloned.1.call-update) | async-done | bytes 33554448 | tf_op jit(solution)/shard_map/all_gather | solution.py:134
  428.4 10.8 fusion.38
  439.2 11.3 fusion.36
  450.5 110.6 %all-gather.17.cloned.1.call-done = bf16[4096,2048]{1,0:T(8,128)(2,1)} async-done(((bf16[4096,128]{1,0:T(8,128)(2,1)}), bf16[4096,2048]{1,0:T(8,128)(2,1)}) %all-gather.17.cloned.1.call-update) | async-done | bytes 16777232 | tf_op jit(solution)/shard_map/all_gather | solution.py:136
  561.1 12.5 multiply_convert_fusion
  573.7 13.1 fusion.35
  586.8 13.8 fusion.68
  600.8 32.4 %all-reduce.8.cloned.1.call-done = bf16[192,2048]{1,0:T(8,128)(2,1)} async-done(((bf16[192,2048]{1,0:T(8,128)(2,1)}), bf16[192,2048]{1,0:T(8,128)(2,1)}) %all-reduce.8.cloned.1.call-update) | async-done | bytes 786448 | tf_op jit(solution)/shard_map/psum | solution.py:223
  642.8 92.5 %while.48 = (s32[]{:T(128)}, f32[192,4,4,64]{0,3,2,1:T(8,128)}, f32[6,512,512]{2,1,0:T(8,128)}, bf16[6,512,512]{1,2,0:T(8,128)(2,1)}, s32[6]{0:T(128)S(1)}, /*in...) while((s32[]{:T(128)}, f32[192,4,4,64]{0,3,2,1:T(8,128)}, ...), condition=%wide.region_23.24_spmd.clone, body=%wide.region_20.23_spmd.clone.sunk | while | flops 1026794432 | bytes 42032584 | solution.py:274
  738.2 11.6 convolution_convert_fusion
  749.8 13.8 convolution_bitcast_fusion.1
  773.4 4.7 fusion.53
  778.1 42.7 %reduce-scatter.4.cloned.1.call-done = f32[192,512]{1,0:T(8,128)} async-done(((f32[3072,512]{1,0:T(8,128)}), f32[192,512]{1,0:T(8,128)}) %reduce-scatter.4.cloned.1.call-update) | async-done | bytes 393232 | tf_op jit(solution)/shard_map/reduce_scatter | solution.py:278
  826.7 6.4 fusion.69
  833.1 27.2 %pad_maximum_fusion.1 = f32[2048,5120]{0,1:T(8,128)} fusion(f32[2048,4096]{0,1:T(8,128)} %convolution_bitcast_fusion.1, f32[2048,1024]{0,1:T(8,128)} %fusion.53), kind=kLoop, calls=%fused_computation.64 | loop fusion | flops 10485760 | bytes 83886080 | tf_op jit(solution)/shard_map/concatenate | solution.py:323
  861.5 14.8 fusion.72
  876.3 13.2 fusion.71
  889.5 8.0 fusion.56
  897.5 63.3 %pad_maximum_fusion = f32[2048,9728]{1,0:T(8,128)} fusion(f32[2048,4096]{1,0:T(8,128)} %fusion.72, f32[2048,4096]{1,0:T(8,128)} %fusion.71, f32[2048,1536]{1,0:T(8,128)} %fusion.56), kind=kLoop, calls=%fused_computation.63 | loop fusion | flops 39845888 | bytes 159383552 | tf_op jit(solution)/shard_map/concatenate | solution.py:308
  963.2 43.9 %all-reduce = (f32[2048]{0:T(1024)}, f32[64]{0:T(128)}, f32[64]{0:T(128)}, f32[2048]{0:T(1024)}) all-reduce(f32[2048]{0:T(1024)S(1)} %get-tuple-element.658, f32[64]{0:T(128)S(1)} %reduce_sum.234, f32[64]{0:T(128)S(1)} %reduce_sum.237, f32[2048]{0:T(1024)S(1)} %copy-done.33), channel_id=1, replica_groups=mesh['ctx'=16,'tp'=2] {'ctx','tp'}, use_global_device_ids=true, to_apply=%region_30.31 | all-reduce | flops 4224 | bytes 33792 | tf_op jit(solution)/shard_map/psum | solution.py:330
  1010.9 278.9 %reduce-scatter.8.cloned.1.call-done = f32[128,5120]{0,1:T(8,128)} async-done(((f32[2048,5120]{0,1:T(8,128)}), f32[128,5120]{0,1:T(8,128)}) %reduce-scatter.8.cloned.1.call-update) | async-done | bytes 2621456 | tf_op jit(solution)/shard_map/reduce_scatter | solution.py:322
  1294.7 734.7 %reduce-scatter.6.cloned.1.call-done = f32[128,9728]{1,0:T(8,128)} async-done(((f32[2048,9728]{1,0:T(8,128)}), f32[128,9728]{1,0:T(8,128)}) %reduce-scatter.6.cloned.1.call-update) | async-done | bytes 4980752 | tf_op jit(solution)/shard_map/reduce_scatter | solution.py:307
  2033.0 4.7 fusion.66
  (448 shorter events, 230.9 us)
Async XLA Ops:
  7.2 68.3 %all-gather.7.cloned.1.call-start = ((), (), s32[]{:S(2)}) async-start(), calls=%async_computation.3 | async-start | bytes 6684672 | tf_op jit(solution)/shard_map/all_gather | solution.py:133
  9.1 111.2 %all-gather.11.cloned.1.call-start = ((), (), s32[]{:S(2)}) async-start(), calls=%async_computation.5 | async-start | bytes 1671168 | tf_op jit(solution)/shard_map/all_gather | solution.py:173
  11.3 68.7 %copy-start.34 = (f32[192]{0:T(256)}, f32[192]{0:T(256)S(1)}, u32[]{:S(2)}) copy-start(f32[192]{0:T(256)S(1)} %add_rsqrt_fusion.3) | copy-start | bytes 2308
  12.1 75.0 %copy-start.23 = (f32[192,32]{0,1:T(8,128)}, f32[192,32]{0,1:T(8,128)S(1)}, u32[]{:S(2)}) copy-start(f32[192,32]{0,1:T(8,128)S(1)} %get-tuple-element.753) | copy-start | bytes 73732
  12.1 68.1 %copy-start.36 = (f32[64]{0:T(128)S(1)}, f32[64]{0:T(128)}, u32[]{:S(2)}) copy-start(f32[64]{0:T(128)} %param.26) | copy-start | bytes 772
  81.8 85.4 %all-gather.9.cloned.1.call-start = ((), (), s32[]{:S(2)}) async-start(), calls=%async_computation.4 | async-start | bytes 3342336 | tf_op jit(solution)/shard_map/all_gather | solution.py:190
  83.5 137.8 %all-gather.13.cloned.1.call-start = ((), (), s32[]{:S(2)}) async-start(), calls=%async_computation.6 | async-start | bytes 4456448 | tf_op jit(solution)/shard_map/all_gather | solution.py:135
  84.1 174.1 %all-reduce.6.cloned.1.call-start = ((), (), s32[]{:S(2)}) async-start(), calls=%async_computation.7 | async-start | bytes 1572864 | tf_op jit(solution)/shard_map/psum | solution.py:193
  86.8 33.5 %copy-start.25 = (s32[4]{0:T(128)S(1)}, s32[4]{0:T(128)}, u32[]{:S(2)}) copy-start(s32[4]{0:T(128)} %param.32) | copy-start | bytes 52
  86.8 33.5 %copy-start.27 = (f32[192,16]{0,1:T(8,128)}, f32[192,16]{0,1:T(8,128)S(1)}, u32[]{:S(2)}) copy-start(f32[192,16]{0,1:T(8,128)S(1)} %add_rsqrt_fusion) | copy-start | bytes 36868
  206.5 18.9 copy-start.14
  206.6 18.9 copy-start.12
  225.5 202.9 %all-gather.15.cloned.1.call-start = ((), (), s32[]{:S(2)}) async-start(), calls=%async_computation.8 | async-start | bytes 35651584 | tf_op jit(solution)/shard_map/all_gather | solution.py:134
  228.3 29.9 %copy-start = (bf16[192,2048]{1,0:T(8,128)(2,1)S(1)}, bf16[192,2048]{1,0:T(8,128)(2,1)}, u32[]{:S(2)}) copy-start(bf16[192,2048]{1,0:T(8,128)(2,1)} %param.20) | copy-start | bytes 2359300
  228.3 31.4 %copy-start.30 = (f32[2048]{0:T(1024)S(1)}, f32[2048]{0:T(1024)}, u32[]{:S(2)}) copy-start(f32[2048]{0:T(1024)} %param.28) | copy-start | bytes 24580
  228.3 332.8 %all-gather.17.cloned.1.call-start = ((), (), s32[]{:S(2)}) async-start(), calls=%async_computation.9 | async-start | bytes 17825792 | tf_op jit(solution)/shard_map/all_gather | solution.py:136
  229.1 404.1 %all-reduce.8.cloned.1.call-start = ((), (), s32[]{:S(2)}) async-start(), calls=%async_computation.10 | async-start | bytes 1572864 | tf_op jit(solution)/shard_map/psum | solution.py:223
  261.2 178.0 %copy-start.5 = (bf16[192,2048]{1,0:T(8,128)(2,1)}, bf16[192,2048]{1,0:T(8,128)(2,1)S(1)}, u32[]{:S(2)}) copy-start(bf16[192,2048]{1,0:T(8,128)(2,1)S(1)} %multiply_convert_fusion.3) | copy-start | bytes 2359300
  439.2 121.9 %copy-start.9 = (bf16[192,2048]{1,0:T(8,128)(2,1)S(1)}, bf16[192,2048]{1,0:T(8,128)(2,1)}, u32[]{:S(2)}) copy-start(bf16[192,2048]{1,0:T(8,128)(2,1)} %param.33) | copy-start | bytes 2359300
  586.8 46.4 %copy-start.1 = (bf16[192,2048]{1,0:T(8,128)(2,1)S(1)}, bf16[192,2048]{1,0:T(8,128)(2,1)}, u32[]{:S(2)}) copy-start(bf16[192,2048]{1,0:T(8,128)(2,1)} %all-reduce.6.cloned.1.call-done) | copy-start | bytes 2359300
  600.6 220.2 %reduce-scatter.4.cloned.1.call-start = ((), (), s32[]{:S(2)}) async-start(), calls=%async_computation.11 | async-start | bytes 6684672 | tf_op jit(solution)/shard_map/reduce_scatter | solution.py:278
  735.3 225.6 %all-reduce.10.cloned.1.call-start = ((), (), s32[]{:S(2)}) async-start(), calls=%async_computation.14 | async-start | bytes 3145728 | tf_op jit(solution)/shard_map/psum | solution.py:203
  749.8 13.9 copy-start.24
  749.8 13.9 copy-start.26
  773.4 50.1 %copy-start.16 = (f32[192,256]{0,1:T(8,128)S(1)}, f32[192,256]{0,1:T(8,128)}, u32[]{:S(2)}) copy-start(f32[192,256]{0,1:T(8,128)} %copy-done.15) | copy-start | bytes 589828
  778.1 48.6 %copy-start.18 = (bf16[192,1024]{1,0:T(8,128)(2,1)S(1)}, bf16[192,1024]{1,0:T(8,128)(2,1)}, u32[]{:S(2)}) copy-start(bf16[192,1024]{1,0:T(8,128)(2,1)} %get-tuple-element.734) | copy-start | bytes 1179652
  833.1 456.7 %reduce-scatter.8.cloned.1.call-start = ((), (), s32[]{:S(2)}) async-start(), calls=%async_computation.13 | async-start | bytes 44564480 | tf_op jit(solution)/shard_map/reduce_scatter | solution.py:322
  860.4 1169.0 %reduce-scatter.6.cloned.1.call-start = ((), (), s32[]{:S(2)}) async-start(), calls=%async_computation.12 | async-start | bytes 84672512 | tf_op jit(solution)/shard_map/reduce_scatter | solution.py:307
  861.5 14.8 copy-start.21
  876.3 13.2 copy-start.29
  876.3 13.2 copy-start.35
  960.8 46.3 %copy-start.11 = (bf16[192,2048]{1,0:T(8,128)(2,1)S(1)}, bf16[192,2048]{1,0:T(8,128)(2,1)}, u32[]{:S(2)}) copy-start(bf16[192,2048]{1,0:T(8,128)(2,1)} %param.33) | copy-start | bytes 2359300
  (20 other events, 82.7 us)
Sparse Core Ops, SparseCore 0:
  10.9 64.5 all-gather.6
  82.0 38.2 all-gather.10
  123.1 44.0 all-gather.8
  169.3 52.0 all-gather.12
  225.6 32.5 all-reduce.5
  260.3 168.0 all-gather.14
  430.8 130.3 all-gather.16
  600.7 32.4 all-reduce.7
  735.5 85.2 reduce-scatter.3
  833.2 50.8 all-reduce.9
  888.3 401.4 reduce-scatter.7
  1293.9 735.4 reduce-scatter.5
where the time goes:
time: 2050 us; the launch traced here: 2040 us
  waiting for transfers between devices  1520 us (74%)
  matrix products  240 us (12%)
  other arithmetic  151 us (7%)
  local copies, waits for them, and re-layouts  75.4 us (4%)
  blocking collectives  43.9 us (2%)
    reduce_scatter x1, waiting for transfers between devices, shards(): lax.psum_scatter(jnp.concatenate([transposed_times(left_one, grad_proj),...  735 us
    reduce_scatter x1, waiting for transfers between devices, shards(): lax.psum_scatter(jnp.concatenate([transposed_times(left_one, mixed_low),...  279 us
    all_gather x1, waiting for transfers between devices, shards(): lax.all_gather(paired, 'ctx', axis=1, tiled=True)  167 us
    all_gather x1, waiting for transfers between devices, shards(): lax.all_gather(down_weight, 'ctx', axis=1, tiled=True)  111 us
    all_gather x1, waiting for transfers between devices, shards(): lax.all_gather(united_rows, 'ctx', axis=0, tiled=True)  63.4 us
    concatenate x1, other arithmetic, shards(): jnp.concatenate([transposed_times(left_one, grad_proj), transposed_times(...  63.3 us
    dot_general x5, matrix products, transposed_times(): lax.dot_general(left_side, right_side, (((0,), (0,)), ((), ())), preferre...  54.5 us
    dot_general x5, matrix products, times_transposed(): lax.dot_general(left_side, right_side, (((1,), (1,)), ((), ())), preferre...  49.9 us
  transfers between devices with their start and end apart: 12, of which 11 were waited for; matrix products, arithmetic and copies ran while one was open for 14% of the time, Pallas kernels for 0%

commit v1 on v0

v1 whole, which is shorter than its diff:
```python
import functools

import jax
import jax.numpy as jnp
from jax import lax
from jax.experimental import pallas as pl
from jax.experimental.pallas import tpu as pltpu
from jax.sharding import Mesh
from jax.sharding import PartitionSpec as P

epsilon = 1e-05
rope_base = 1000000.0
RING = 4
QUARTERS = 4
ORDER = (1, 2, 3, 0)
LOG2E = 1.4426950408889634
NEG = -1e30
PAIR = 2
DEPTH = {"a": 2, "b": 1, "tp": 1}
bf16 = jnp.bfloat16
f32 = jnp.float32


def norm_rows(values):
    inverse = lax.rsqrt(jnp.mean(values * values, axis=-1, keepdims=True) + epsilon)
    return values * inverse, inverse


def norm_back(grad_out, gain, unit_rows, inverse):
    scaled = grad_out * gain
    inner_mean = jnp.mean(scaled * unit_rows, axis=-1, keepdims=True)
    return inverse * (scaled - unit_rows * inner_mean)


def dot(left, right, left_dim, right_dim):
    return lax.dot_general(
        left, right, (((left_dim,), (right_dim,)), ((), ())), preferred_element_type=f32
    )


class Links:
    def __init__(self):
        self.sent = {}

    def send(self, link, values, move):
        sent = self.sent.setdefault(link, [])
        if len(sent) >= DEPTH[link]:
            values = lax.optimization_barrier((*values, *sent[-DEPTH[link]]))[: len(values)]
        sent.append(tuple(move(i, value) for i, value in enumerate(values)))
        return sent[-1]


links = Links()


def ring_permute(value, step):
    return lax.ppermute(value, "a", [(i, (i + step) % RING) for i in range(RING)])


def ring_shift(value, step):
    return links.send("a", [value], lambda _, v: ring_permute(v, step))[0]


def swap(value, axis):
    def move(_, v):
        return lax.ppermute(v, axis, [(0, 1), (1, 0)])

    return move(0, value) if axis == "core" else links.send(axis, [value], move)[0]


def after(value, *events):
    return lax.optimization_barrier((value,) + events)[0]


def after_all(values, *events):
    return list(lax.optimization_barrier((*values, *events))[: len(values)])


def window(buffer, index):
    start = [0 if i is None else i for i in index] + [0] * (buffer.ndim - len(index))
    shape = [buffer.shape[d] if i is None else 1 for d, i in enumerate(index)]
    return start, shape + list(buffer.shape[len(index) :])


def put(buffer, value, *index):
    start, shape = window(buffer, index)
    return lax.dynamic_update_slice(buffer, value.reshape(shape), start)


def take(buffer, *index):
    start, shape = window(buffer, index)
    kept = [buffer.shape[d] for d, i in enumerate(index) if i is None]
    return lax.dynamic_slice(buffer, start, shape).reshape(kept + list(buffer.shape[len(index) :]))


class Place:
    def __init__(self, count):
        self.a, self.b, self.core, self.x = (lax.axis_index(n) for n in ("a", "b", "core", "tp"))
        self.count = count

    def back(self, k):
        return (self.a - k) % RING

    def ahead(self, k):
        return (self.a + k) % RING

    def assembled(self, pieces):
        own = jnp.zeros((RING,) + pieces[0].shape, pieces[0].dtype)
        for k in range(RING):
            own = put(own, pieces[k], self.back(k))
        return own.reshape(-1, own.shape[-1])

    def over_b_rows(self, own):
        return swap(own, "b")

    def offsets(self, width):
        quarter = width // QUARTERS
        first = self.b if self.count == 2 else 0
        return [(c * 2 + h) * quarter for c in (self.core, 1 - self.core) for h in (first, 1 - first)]

    def over_b(self, array):
        if self.count == 2:
            theirs = swap(take(array, 1 - self.b).astype(bf16), "b")
            return take(array, self.b) + theirs.astype(f32)
        return lax.psum_scatter(array.astype(bf16), "b", scatter_dimension=0, tiled=False).astype(f32)

    def sum_everywhere(self, value):
        def tree(values):
            while len(values) > 1:
                values = [values[i] + values[i + 1] for i in range(0, len(values), 2)]
            return values[0]

        value = value + swap(value, "core")
        if self.count == 2:
            axes = ("b", "tp")
            value = tree([value] + [lax.ppermute(value, axes, [(i, i ^ m) for i in range(4)]) for m in (1, 2, 3)])
        else:
            value = lax.psum(value, "b")
            value = value + lax.ppermute(value, "tp", [(0, 1), (1, 0)])
        return tree([value] + [lax.ppermute(value, "a", [(i, i ^ m) for i in range(RING)]) for m in range(1, RING)])


class RowGather:
    def __init__(self, own, other=None):
        self.mine, self.other = [own], [] if other is None else [other]

    def ring(self, *due):
        self.mine.append(ring_shift(after(self.mine[-1], *due) if due else self.mine[-1], 1))

    def cross(self):
        self.other.append(swap(self.mine[len(self.other)], "tp"))

    def all(self):
        for _ in range(1, RING):
            self.ring()
            self.cross()
        if len(self.other) < RING:
            self.cross()
        return self

    def chunks(self):
        return list(zip(self.mine, self.other))


class RowScatter:
    def __init__(self):
        self.totals, self.theirs, self.arrived = [], [], []

    def cross(self, mine, other):
        self.theirs.append(swap(other, "tp"))
        self.totals.append(mine.astype(f32) + self.theirs[-1].astype(f32))

    def ring(self):
        n = len(self.arrived)
        self.arrived.append(ring_shift(self.sum(n).astype(bf16), 1))

    def sum(self, n):
        return self.totals[n] + self.arrived[n - 1].astype(f32) if n else self.totals[0]


class Exchange:
    def __init__(self, at, parts):
        self.at, self.parts, self.got, self.hop = at, parts, [take(parts, at.a), None, None, None], None

    def piece(self, k):
        return take(self.parts, self.at.ahead(k))

    def step(self, k):
        if k != 2:
            self.got[k] = ring_shift(self.piece(k), k)
            return
        if self.hop is None:
            self.hop = ring_shift(self.piece(2), 1)
        else:
            self.got[2] = ring_shift(self.hop, 1)

    def steps(self):
        for k in (1, 3, 2, 2):
            self.step(k)
        return [self.got[1], self.got[3], self.hop, self.got[2]]

    def whole(self):
        got = links.send("a", [self.piece(k) for k in (1, 2, 3)], lambda i, v: ring_permute(v, i + 1))
        self.got[1:] = got
        return self.got


def lay_kernel(turned, place_ref, *refs):
    pieces, out_ref = refs[:-1], refs[-1]
    for k, piece in enumerate(pieces):

        @pl.when(pl.program_id(0) == k)
        def _(piece=piece):
            value = piece[...].astype(f32)
            out_ref[...] = value.T if turned else value


def lay(pieces, a, first, n, turned):
    rows = pieces[0].shape[0]
    block = first // n
    place = a
    if turned:
        shape, spec = (RING * n, rows), pl.BlockSpec((n, rows), lambda k, p: ((p[0] + RING - k) % RING, 0))
    else:
        shape, spec = (rows, RING * n), pl.BlockSpec((rows, n), lambda k, p: (0, (p[0] + RING - k) % RING))
    return pl.pallas_call(
        functools.partial(lay_kernel, turned),
        grid_spec=pltpu.PrefetchScalarGridSpec(
            num_scalar_prefetch=1,
            grid=(RING,),
            in_specs=[pl.BlockSpec((rows, n), lambda k, p: (0, block))] * RING,
            out_specs=spec,
        ),
        out_shape=jax.ShapeDtypeStruct(shape, f32),
        cost_estimate=pl.CostEstimate(flops=0, bytes_accessed=rows * n * RING * 6, transcendentals=0),
    )(place, *pieces)


A, B, CORE, X, DOC = range(5)


class Chunk:
    def __init__(self, info_ref, k, count, tok):
        self.info, self.count, self.tok = info_ref, count, tok
        self.ring = lax.rem(info_ref[A] + RING - k, RING)
        self.first = ((self.ring * count + info_ref[B]) * 2 + info_ref[CORE]) * tok
        self.shift = info_ref[X] * (tok // 2)

    def docs(self):
        return [self.info[DOC + i] for i in range(self.info.shape[0] - DOC)]

    def begin(self, place):
        best = place * 0
        for d in self.docs():
            best = jnp.maximum(best, jnp.where(place >= d, d, 0))
        return best

    def places(self, shape, dim):
        n = lax.broadcasted_iota(jnp.int32, shape, dim)
        n = lax.rem(n, self.tok)
        return self.first + n + jnp.where(n < self.tok // 2, self.shift, -self.shift)

    def keys(self, first_key, n):
        row = lax.broadcasted_iota(jnp.int32, (n, 1), 0)
        within = lax.rem(row, self.tok)
        return first_key + row + jnp.where(within < self.tok // 2, self.shift, -self.shift)

    def quarter(self, i, quarter):
        core = self.info[CORE] if i < 2 else 1 - self.info[CORE]
        side = self.info[B] if self.count == 2 else 0
        side = side if i % 2 == 0 else 1 - side
        return pl.ds(pl.multiple_of((core * 2 + side) * quarter, quarter), quarter)


def row_quarter(at, mine_ref, other_ref, i, quarter):
    cols = at.quarter(i, quarter)
    return jnp.concatenate([mine_ref[:, cols], other_ref[:, cols]], axis=0)


def store_quarter(at, mine_ref, other_ref, i, value):
    half, quarter = value.shape[0] // 2, value.shape[1]
    cols = at.quarter(i, quarter)
    value = value.astype(mine_ref.dtype)
    mine_ref[:, cols] = value[:half]
    other_ref[:, cols] = value[half:]


def rotate(values, cosine, sine):
    half = values.shape[1] // 2
    first, second = values[:, :half], values[:, half:]
    return jnp.concatenate([first * cosine - second * sine, second * cosine + first * sine], axis=1)


def head_norm(values):
    inverse = lax.rsqrt(jnp.mean(values * values, axis=1, keepdims=True) + epsilon)
    return values * inverse, inverse


def head_norm_back(grad_out, gain, unit, inverse):
    scaled = grad_out * gain
    inner_mean = jnp.mean(scaled * unit, axis=1, keepdims=True)
    return inverse * (scaled - unit * inner_mean)


def heads_to_lanes(array, head):
    return jnp.concatenate([array[i : i + head] for i in range(0, array.shape[0], head)], axis=1)


def lanes_to_heads(array, tok):
    return jnp.concatenate([array[:, i : i + tok] for i in range(0, array.shape[1], tok)], axis=0)


def project_kernel(k, count, info_ref, mine_ref, other_ref, w0, w1, w2, w3, qg_ref, kg_ref, q_ref, kv_ref, raw_ref, cos_ref, sin_ref):
    head = qg_ref.shape[0]
    tok = cos_ref.shape[1]
    at = Chunk(info_ref, k, count, tok)
    place = at.places((1, tok), 1)
    turn = lax.broadcasted_iota(jnp.int32, (head // 2, 1), 0).astype(f32) * (2.0 / head)
    turned = (1.0 / rope_base**turn) * (place - at.begin(place)).astype(f32)
    cos_ref[...] = jnp.cos(turned)
    sin_ref[...] = jnp.sin(turned)
    q_n = q_ref.shape[0]
    total = 0.0
    for i, w in enumerate((w0, w1, w2, w3)):
        rows = row_quarter(at, mine_ref, other_ref, i, w.shape[0])
        total = total + jnp.dot(rows, w[:, : raw_ref.shape[0]], preferred_element_type=f32)
    raw = total.T
    raw_ref[...] = raw
    cosine, sine = cos_ref[...], sin_ref[...]
    q_unit, _ = head_norm(raw[:q_n].reshape(q_n // head, head, tok))
    q_ref[...] = rotate(q_unit * qg_ref[...], cosine, sine).reshape(q_n, tok).astype(bf16)
    k_unit, _ = head_norm(raw[q_n + head :].reshape(1, head, tok))
    key = rotate(k_unit * kg_ref[...], cosine, sine).reshape(head, tok)
    kv_ref[...] = jnp.concatenate([raw[q_n : q_n + head], key], axis=0).T.astype(bf16)


def key_loop(at, lanes, step):
    size = PAIR * at.tok
    place = at.places((1, lanes), 1)
    start = at.begin(place)
    high = at.begin(at.first + at.tok - 1)

    def masked(j, scores):
        key = at.keys(j * size, size)
        return jnp.where((key <= place) & (key >= start), scores, NEG)

    def body(j, carry):
        need = ((j + 1) * size > at.first) | (j * size < high)
        pl.when(need)(lambda: step(j, masked))
        pl.when(jnp.logical_not(need))(lambda: step(j, lambda j, scores: scores))
        return carry

    lax.fori_loop(at.begin(at.first) // size, (at.first + at.tok + size - 1) // size, body, 0)


def key_rows(kv_ref, j):
    return kv_ref[pl.ds(j * PAIR, PAIR)].reshape(PAIR * kv_ref.shape[1], kv_ref.shape[2])


def attend_kernel(
    scale, k, count, info_ref, q_ref, kv_ref, w0, w1, w2, w3,
    mixed_ref, lse_ref, low_ref, mine_ref, other_ref, acc, total
):
    head = kv_ref.shape[2] // 2
    tok = q_ref.shape[1]
    at = Chunk(info_ref, k, count, tok)
    acc[...] = jnp.zeros_like(acc)
    total[...] = jnp.zeros_like(total)
    q = heads_to_lanes(q_ref[...], head)
    q = jnp.concatenate([jnp.zeros_like(q), q], axis=0)
    size = PAIR * tok

    def step(j, masked):
        kv = key_rows(kv_ref, j)
        scores = jnp.dot(kv, q, preferred_element_type=f32) * (scale * LOG2E)
        scores = masked(j, scores)
        weights = jnp.exp2(scores)
        total[...] += jnp.sum(weights.reshape(size // 8, 8, -1), axis=0)
        acc[...] += lax.dot_general(
            kv, weights.astype(bf16), (((0,), (0,)), ((), ())), preferred_element_type=f32
        )

    key_loop(at, q.shape[1], step)
    row_total = jnp.sum(total[...], axis=0, keepdims=True)
    lse_ref[...] = jnp.log2(row_total)
    mixed = acc[0:head, :] / row_total
    mixed_ref[...] = mixed
    low = lanes_to_heads(mixed, tok).T.astype(bf16)
    low_ref[...] = low
    for i, w in enumerate((w0, w1, w2, w3)):
        store_quarter(at, mine_ref, other_ref, i, dot(low, w[:, w.shape[1] - low.shape[1] :], 1, 1))


def attend_back_kernel(
    scale, k, count, info_ref, gm_ref, go_ref, w0, w1, w2, w3, q_ref, kv_ref, lse_ref, mixed_ref,
    raw_ref, cos_ref, sin_ref, qg_ref, dkv_in, gq_ref, gain_ref, dkv, acc
):
    head = kv_ref.shape[2] // 2
    q_n, tok = q_ref.shape
    at = Chunk(info_ref, k, count, tok)
    acc[...] = jnp.zeros_like(acc)
    if dkv_in is None:
        dkv[...] = jnp.zeros_like(dkv)
    else:
        dkv[...] = dkv_in[...]
    total = 0.0
    for i, w in enumerate((w0, w1, w2, w3)):
        rows = row_quarter(at, gm_ref, go_ref, i, w.shape[0])
        total = total + jnp.dot(rows, w[:, w.shape[1] - q_n :], preferred_element_type=f32)
    g = heads_to_lanes(total.T.astype(bf16), head)
    delta = jnp.sum(g.astype(f32) * mixed_ref[...], axis=0, keepdims=True)
    g = jnp.concatenate([g, jnp.zeros_like(g)], axis=0)
    q = heads_to_lanes(q_ref[...], head)
    q = jnp.concatenate([jnp.zeros_like(q), q], axis=0)
    lse = lse_ref[...]
    size = PAIR * tok

    def step(j, masked):
        kv = key_rows(kv_ref, j)
        scores = jnp.dot(kv, q, preferred_element_type=f32) * (scale * LOG2E)
        scores = masked(j, scores)
        probs = jnp.exp2(scores - lse)
        grad_probs = jnp.dot(kv, g, preferred_element_type=f32)
        grad_scores = (probs * (grad_probs - delta)).astype(bf16)
        grad_kv = dot(probs.astype(bf16), g, 1, 1) + dot(grad_scores, q, 1, 1)
        dkv[pl.ds(j * PAIR, PAIR)] += grad_kv.reshape(PAIR, tok, -1)
        acc[...] += lax.dot_general(
            kv, grad_scores, (((0,), (0,)), ((), ())), preferred_element_type=f32
        )

    key_loop(at, q.shape[1], step)
    grad = lanes_to_heads(acc[head:, :] * scale, tok).reshape(q_n // head, head, tok)
    grad = rotate(grad, cos_ref[...], -sin_ref[...])
    unit, inverse = head_norm(raw_ref[0:q_n].reshape(q_n // head, head, tok))
    gain_ref[...] = jnp.sum(grad * unit, axis=0)
    gq_ref[...] = head_norm_back(grad, qg_ref[...], unit, inverse).reshape(q_n, tok).T.astype(bf16)


def first_back(*refs):
    attend_back_kernel(*refs[:18], None, *refs[18:])


def project_back_kernel(
    scale, k, count, info_ref, gkv_ref, gq_ref, raw_ref, cos_ref, sin_ref, kg_ref, w0, w1, w2, w3,
    gproj_ref, gain_ref, mine_ref, other_ref
):
    head = kg_ref.shape[0]
    tok, q_n = gq_ref.shape
    at = Chunk(info_ref, k, count, tok)
    gkv = gkv_ref[...].T
    grad = rotate((gkv[head:] * scale).reshape(1, head, tok), cos_ref[...], -sin_ref[...])
    unit, inverse = head_norm(raw_ref[q_n + head : q_n + 2 * head].reshape(1, head, tok))
    gain_ref[...] = jnp.sum(grad * unit, axis=0)
    gk = head_norm_back(grad, kg_ref[...], unit, inverse).reshape(head, tok)
    rest = jnp.concatenate([gkv[:head], gk], axis=0).T.astype(bf16)
    gproj = jnp.concatenate([gq_ref[...], rest], axis=1)
    gproj_ref[...] = gproj
    for i, w in enumerate((w0, w1, w2, w3)):
        store_quarter(at, mine_ref, other_ref, i, dot(gproj, w[:, : gproj.shape[1]], 1, 1))


def feed_kernel(
    k, count, step, info_ref, hm_ref, ho_ref, cm_ref, co_ref,
    p0, p1, p2, p3, d0, d1, d2, d3, *refs
):
    act_ref, sm_ref, so_ref, bm_ref, bo_ref, h_rows, c_rows, *turned = refs[-10:]
    half = hm_ref.shape[0]
    at = Chunk(info_ref, k, count, 2 * half)
    quarter, width = d0.shape
    pairs, downs = (p0, p1, p2, p3), (d0, d1, d2, d3)
    for rows, mine_ref, other_ref in ((h_rows, hm_ref, ho_ref), (c_rows, cm_ref, co_ref)):
        rows[0:half] = mine_ref[...]
        rows[half:] = other_ref[...]

    def product(rows, weights, first):
        cols, total = pl.ds(pl.multiple_of(first, step), step), 0.0
        for i, w in enumerate(weights):
            total = total + jnp.dot(rows[:, at.quarter(i, quarter)], w[:, cols], preferred_element_type=f32)
        return total

    def ahead(j, carry):
        cols = pl.ds(pl.multiple_of(j * step, step), step)
        gate, up = product(h_rows, pairs, j * step), product(h_rows, pairs, width + j * step)
        back = product(c_rows, downs, j * step)
        sigmoid = 1.0 / (1.0 + jnp.exp(-gate))
        silu = gate * sigmoid
        hidden = (silu * up).astype(bf16)
        grad_gate = (back * up * sigmoid * (1.0 + gate * (1.0 - sigmoid))).astype(bf16)
        grad_up = (back * silu).astype(bf16)
        for n, (value, turn_ref) in enumerate(zip((grad_gate, grad_up, hidden), turned)):
            act_ref[:, pl.ds(pl.multiple_of(n * width + j * step, step), step)] = value
            turn_ref[cols, :] = value.T
        return carry

    lax.fori_loop(0, width // step, ahead, 0)
    grad_gate, grad_up, hidden = (ref[...] for ref in turned)
    for i in range(QUARTERS):
        second = jnp.dot(pairs[i][:, :width], grad_gate, preferred_element_type=f32)
        second = second + jnp.dot(pairs[i][:, width:], grad_up, preferred_element_type=f32)
        store_quarter(at, sm_ref, so_ref, i, second.T)
        branch = jnp.dot(downs[i][...], hidden, preferred_element_type=f32)
        store_quarter(at, bm_ref, bo_ref, i, branch.T)


def half_rows(ref, x):
    half = ref.shape[0] // 2
    return pl.ds(pl.multiple_of(x * half, half), half)


def reorder(ref, rows, order, width):
    value = ref[rows, :] if rows is not None else ref[...]
    size = width // len(order)
    return jnp.concatenate([value[:, n * size : (n + 1) * size] for n in order], axis=1)


def enter_kernel(order, info_ref, in_ref, gain_ref, own_ref, unit_ref, inverse_ref, low_ref, other_ref):
    width = in_ref.shape[1]
    gain = reorder(gain_ref, None, order, width)
    for x, low in ((info_ref[X], low_ref), (1 - info_ref[X], other_ref)):
        rows = reorder(in_ref, half_rows(in_ref, x), order, width).astype(f32)
        unit, inverse = norm_rows(rows)
        low[...] = (unit * gain).astype(bf16)
        if low is low_ref:
            own_ref[...] = rows
            unit_ref[...] = unit
            inverse_ref[...] = jnp.broadcast_to(inverse, inverse_ref.shape)


def reorder_kernel(order, info_ref, in_ref, one_ref, two_ref, own_ref, other_ref, gain_one_ref, gain_two_ref):
    width = in_ref.shape[1]
    own_ref[...] = reorder(in_ref, half_rows(in_ref, info_ref[X]), order, width)
    other_ref[...] = reorder(in_ref, half_rows(in_ref, 1 - info_ref[X]), order, width)
    gain_one_ref[...] = reorder(one_ref, None, order, width)
    gain_two_ref[...] = reorder(two_ref, None, order, width)


def leave_kernel(order, info_ref, own_ref, other_ref, out_ref):
    width = own_ref.shape[1]
    for x, ref in ((info_ref[X], own_ref), (1 - info_ref[X], other_ref)):
        out_ref[half_rows(out_ref, x), :] = reorder(ref, None, order, width)


def whole(array):
    shape = array.shape
    return pl.BlockSpec(shape, lambda *_: (0,) * len(shape))


def shaped(shape, kind):
    return jax.ShapeDtypeStruct(shape, kind)


def call(kernel, info, operands, results, scratch=(), cost=(0, 0, 0), aliases=None, in_specs=None, out_specs=None, grid=(1,), vmem=20):
    return pl.pallas_call(
        kernel,
        grid_spec=pltpu.PrefetchScalarGridSpec(
            num_scalar_prefetch=1,
            grid=grid,
            in_specs=in_specs or [whole(o) for o in operands],
            out_specs=out_specs or [whole(r) for r in results],
            scratch_shapes=list(scratch),
        ),
        out_shape=results,
        input_output_aliases=aliases or {},
        compiler_params=pltpu.CompilerParams(vmem_limit_bytes=vmem << 20),
        cost_estimate=pl.CostEstimate(
            flops=cost[0], bytes_accessed=cost[1], transcendentals=cost[2]
        ),
    )(info, *operands)


def shards(
    count,
    inputs,
    norm1_gain,
    query_weight,
    key_weight,
    value_weight,
    query_gain,
    key_gain,
    out_weight,
    norm2_gain,
    gate_weight,
    up_weight,
    down_weight,
    doc_starts,
    cotangent,
):
    at = Place(count)
    links.sent.clear()
    tok, width = inputs.shape
    half = tok // 2
    head = query_gain.shape[0]
    q_n = query_weight.shape[1] // RING
    hidden_n = gate_weight.shape[1] // RING
    heads = q_n // head
    assert key_weight.shape[1] // RING == head
    lanes = heads * tok
    scale = head ** (-0.5)
    blocks = RING * count * 2
    rows = width // blocks

    places = [(i, j, c) for c in range(2) for j in range(count) for i in range(RING)]
    to_order = [(i * count + j) * 2 + c for i, j, c in places]
    to_natural = [to_order.index(n) for n in range(blocks)]

    def natural(array):
        array = array.reshape((2, count, RING, rows))
        return jnp.swapaxes(array, 0, 2).reshape(width)

    def pieces(*arrays):
        stacked = []
        for i in range(RING):
            cut = [m[:, i * (m.shape[1] // RING) : (i + 1) * (m.shape[1] // RING)] for m in arrays]
            stacked.append(jnp.concatenate(cut, axis=1))
        return jnp.stack(stacked)

    info = jnp.concatenate([jnp.stack([at.a, at.b, at.core, at.x]).astype(jnp.int32), doc_starts])
    half_low, half_wide = shaped((half, width), bf16), shaped((half, width), f32)
    row_pair = [half_low] * 2
    query_gain, key_gain = query_gain[:, None], key_gain[:, None]
    gains_natural = [norm1_gain[None], norm2_gain[None]]

    def beside(own):
        if count == 2:
            return [own, swap(own, "b")]
        return jnp.split(lax.all_gather(own, "b", axis=0, tiled=True), 2)

    def quarters(near):
        return list(near) + [swap(part, "core") for part in near]

    side_got = Exchange(at, pieces(query_weight, value_weight, key_weight, out_weight.T)).whole()
    in_own, unit_one, scale_one, h1_own, h1_other = call(
        functools.partial(enter_kernel, to_order),
        info,
        [inputs, gains_natural[0]],
        [half_wide, half_wide, shaped((half, 128), f32), half_low, half_low],
    )
    scale_one = scale_one[:, :1]
    rows_one = RowGather(h1_own, h1_other)
    rows_one.ring()
    first_step = rows_one.mine[1]
    side_near = beside(at.assembled(side_got))
    rows_one.cross()
    rows_one.ring()
    side_w = quarters(side_near)
    rows_one.cross()
    rows_one.ring()
    rows_one.cross()
    h1 = rows_one.chunks()
    pair_x = Exchange(at, pieces(after(gate_weight, first_step), up_weight))
    down_x = Exchange(at, pieces(after(down_weight, rows_one.mine[2]).T))
    q, raw, cosine, sine = ([None] * RING for _ in range(4))
    kv_own = jnp.zeros((RING, tok, 2 * head), bf16)
    for k in range(RING):
        q[k], kv_k, raw[k], cosine[k], sine[k] = call(
            functools.partial(project_kernel, k, count),
            info,
            [*h1[k], *side_w, query_gain, key_gain],
            [
                shaped((q_n, tok), bf16),
                shaped((tok, 2 * head), bf16),
                shaped((q_n + 2 * head, tok), f32),
                *[shaped((head // 2, tok), f32)] * 2,
            ],
            cost=(2 * tok * width * (q_n + 2 * head), 3 << 20, 0),
        )
        kv_own = put(kv_own, kv_k, at.back(k))
    pair_x.step(1)
    pair_x.step(3)
    kv_own = after(kv_own, pair_x.got[1])

    pairs = blocks * tok * lanes // 2
    kv = jnp.zeros((RING, count, 2, tok, 2 * head), bf16)
    if count == 2:
        kv_b = jnp.zeros((RING, 2, tok, 2 * head), bf16)
        kv_b = put(put(kv_b, kv_own, None, at.b), swap(kv_own, "b"), None, 1 - at.b)
    else:
        kv_b = lax.all_gather(kv_own, "b", axis=1)
    kv = put(put(kv, kv_b, None, None, at.core), swap(kv_b, "core"), None, None, 1 - at.core)
    kv = kv.reshape(blocks, tok, 2 * head)
    mixed, lse, low = ([None] * RING for _ in range(3))
    attend = RowScatter()
    for n, k in enumerate(ORDER):
        mixed[k], lse[k], low[k], *part = call(
            functools.partial(attend_kernel, scale, k, count),
            info,
            [after(q[k], *attend.theirs[: max(0, n - 1)][-1:], *attend.arrived[: max(0, n - 2)]), kv, *side_w],
            [shaped((head, lanes), f32), shaped((1, lanes), f32), shaped((tok, q_n), bf16), *row_pair],
            [pltpu.VMEM((2 * head, lanes), f32), pltpu.VMEM((8, lanes), f32)],
            (pairs * 2 * head * 8, 3 << 20, pairs),
        )
        attend.cross(*part)
        if n < RING - 1:
            attend.ring()
            if n < 2:
                pair_x.step(2)
    middle = in_own + attend.sum(RING - 1)
    unit_two, scale_two = norm_rows(middle)
    pair_near = beside(at.assembled(pair_x.got))
    cot_own, cot_other, gain_one, gain_two = call(
        functools.partial(reorder_kernel, to_order),
        info,
        [after(cotangent, kv_own), *gains_natural],
        [half_low, half_low] + [shaped((1, width), f32)] * 2,
    )

    down_x.step(1)
    down_x.step(3)
    rows_two = RowGather((unit_two * gain_two).astype(bf16))
    rows_cot = RowGather(cot_own, cot_other)
    rows_two.ring()
    rows_two.cross()
    down_x.step(2)
    down_x.step(2)
    down_near = beside(at.assembled(down_x.got))
    for _ in range(1, RING):
        rows_cot.ring()
        rows_two.cross()
        if len(rows_two.mine) < RING:
            rows_two.ring()
        rows_cot.cross()
    h2, cot = rows_two.chunks(), rows_cot.chunks()
    feed_w = quarters(pair_near) + quarters(down_near)

    step = min(512, hidden_n)
    offsets = at.offsets(width)

    def tokens(parts):
        return jnp.concatenate([piece for k in ORDER for piece in parts[k]], axis=0)

    def in_order(parts):
        return jnp.concatenate([parts[k] for k in ORDER], axis=0)

    def left_quarters(left):
        return [lax.dynamic_slice(left, (0, o), (left.shape[0], width // QUARTERS)) for o in offsets]

    def over_cores(left, right):
        theirs = [swap(dot(part, right, 0, 0).astype(bf16), "core") for part in left[2:]]
        total = [dot(part, right, 0, 0) + t.astype(f32) for part, t in zip(left[:2], theirs)]
        return (total[0], total[1].astype(bf16)), theirs

    def over_b(own, far):
        if count == 2:
            over_b.events.append(swap(far, "b"))
            total = own + over_b.events[-1].astype(f32)
        else:
            both = jnp.concatenate([own.astype(bf16), far], axis=0).reshape(count, RING * rows, -1)
            total = lax.psum_scatter(both, "b", scatter_dimension=0, tiled=False)
        return total.astype(bf16).reshape(RING, rows, -1)

    second = RowScatter()
    branch = [None] * RING
    act = None
    row_specs = [whole(half_low)] * 2
    for n, k in enumerate(ORDER):
        operands = [after(h2[k][0], *second.theirs[: max(0, n - 1)][-1:], *second.arrived[: max(0, n - 2)]), h2[k][1], *cot[k], *feed_w]
        specs, aliases = row_specs * 2 + [pl.BlockSpec(memory_space=pltpu.VMEM)] * (2 * QUARTERS), None
        if act is not None:
            operands.append(act)
            specs = specs + [pl.BlockSpec(memory_space=pl.ANY)]
            aliases = {len(operands): 0}
        act, *part = call(
            functools.partial(feed_kernel, k, count, step),
            info,
            operands,
            [shaped((RING * tok, 3 * hidden_n), bf16), *row_pair, *row_pair],
            [pltpu.VMEM((tok, width), bf16)] * 2 + [pltpu.VMEM((hidden_n, tok), bf16)] * 3,
            (12 * tok * width * hidden_n, 15 << 20, tok * hidden_n),
            aliases,
            specs,
            [pl.BlockSpec((tok, 3 * hidden_n), lambda j, _, n=n: (n, 0))] + row_specs * 2,
        )
        branch[k] = part[2:]
        second.cross(*part[:2])
        if n < RING - 1:
            second.ring()
    h2_q, cot_q = left_quarters(tokens(h2)), left_quarters(tokens(cot))
    act_due = ((), (), ())
    sums, events = [], []
    for n, left in enumerate((h2_q, h2_q, cot_q)):
        both, theirs = over_cores(left, after(act, *act_due[n])[:, n * hidden_n : (n + 1) * hidden_n])
        sums.append(both)
        events.append(theirs)
    grad_second = second.sum(RING - 1)
    over_b.events = []
    gate_own = over_b(*sums[0])

    grad_middle = cot_own.astype(f32) + norm_back(grad_second, gain_two, unit_two, scale_two)
    gain_two_term = jnp.sum(grad_second * unit_two, axis=0)
    rows_att = RowGather(grad_middle.astype(bf16))
    rows_att.all()
    grad_att = rows_att.chunks()
    up_own = over_b(*sums[1])
    down_own = over_b(*sums[2])
    gate_x, up_x, down_x = Exchange(at, gate_own), Exchange(at, up_own), Exchange(at, down_own)
    late = RowScatter()
    grad_kv, gq, q_gain_term = None, [None] * RING, 0.0
    for k in range(RING):
        operands = [after(grad_att[k][0], *([(), (), *[(e,) for e in over_b.events[:2]]] if count == 2 else [()] * RING)[k]), grad_att[k][1], *side_w, q[k], kv, lse[k], mixed[k], raw[k], cosine[k], sine[k], query_gain]
        kernel, aliases = first_back, None
        if grad_kv is not None:
            kernel, aliases = attend_back_kernel, {len(operands) + 1: 2}
            operands.append(grad_kv)
        gq[k], term, grad_kv = call(
            functools.partial(kernel, scale, k, count),
            info,
            operands,
            [shaped((tok, q_n), bf16), shaped((head, tok), f32), shaped((blocks, tok, 2 * head), f32)],
            [pltpu.VMEM((2 * head, lanes), f32)],
            (pairs * 2 * head * 20, 6 << 20, pairs),
            aliases,
            vmem=20 if blocks * tok <= 4096 else 48,
        )
        q_gain_term = q_gain_term + term
        late.cross(*branch[ORDER[k]])
    gate_due, up_due = gate_x.steps(), up_x.steps()
    for _ in range(RING - 1):
        late.ring()

    grad_kv = after(grad_kv, *over_b.events[2:3]).reshape(RING, count, 2, tok, 2 * head)
    theirs = swap(take(grad_kv, None, None, 1 - at.core).astype(bf16), "core")
    grad_kv = take(grad_kv, None, None, at.core) + theirs.astype(f32)
    if count == 2:
        theirs = swap(take(grad_kv, None, 1 - at.b).astype(bf16), "b")
        grad_kv = take(grad_kv, None, at.b) + theirs.astype(f32)
    else:
        grad_kv = lax.psum_scatter(grad_kv.astype(bf16), "b", scatter_dimension=1, tiled=False).astype(f32)
    out_sum, _ = over_cores(left_quarters(tokens(grad_att)), in_order(low))
    out_own = over_b(*out_sum)
    gproj, k_gain_term = [None] * RING, 0.0
    first = RowScatter()
    for n, k in enumerate(ORDER):
        gproj[k], term, *part = call(
            functools.partial(project_back_kernel, scale, k, count),
            info,
            [take(grad_kv, at.back(k)), gq[k], raw[k], cosine[k], sine[k], key_gain, *side_w],
            [shaped((tok, q_n + 2 * head), bf16), shaped((head, tok), f32), *row_pair],
            cost=(2 * tok * width * (q_n + 2 * head), 3 << 20, 0),
        )
        first.cross(*part)
        k_gain_term = k_gain_term + term
        if n < RING - 1:
            first.ring()
    down_x.steps()
    proj_sum, _ = over_cores(left_quarters(tokens([(after(m, gq[0]), o) for m, o in h1])), in_order(gproj))
    out_got = Exchange(at, out_own).whole()
    proj_got = Exchange(at, over_b(*proj_sum)).whole()

    def leave(own):
        return call(
            functools.partial(leave_kernel, to_natural), info, [own, swap(own, "tp")], [shaped((tok, width), bf16)]
        )[0]

    output = leave((middle + late.sum(RING - 1)).astype(bf16))
    grad_first = first.sum(RING - 1)
    input_grad = (grad_middle + norm_back(grad_first, gain_one, unit_one, scale_one)).astype(bf16)
    gain_one_term = jnp.sum(grad_first * unit_one, axis=0)
    gains = at.sum_everywhere(
        jnp.concatenate([gain_one_term, gain_two_term, jnp.sum(q_gain_term, axis=1), jnp.sum(k_gain_term, axis=1)])
    )
    input_grad = leave(input_grad)
    proj_all = at.assembled(proj_got).reshape(RING, rows, -1)

    def held(values, event):
        return [values[0], *after_all(values[1:], event)]

    def side(first_col, n):
        return jnp.concatenate([proj_all[i, :, first_col : first_col + n] for i in range(RING)], axis=1).astype(f32)

    return (
        output,
        input_grad,
        natural(gains[:width]),
        side(0, q_n),
        side(q_n + head, head),
        side(q_n, head),
        gains[2 * width : 2 * width + head],
        gains[2 * width + head :],
        lay(held(out_got, first.arrived[2]), info, 0, q_n, True),
        natural(gains[width : 2 * width]),
        lay(held(gate_x.got, first.arrived[2]), info, 0, hidden_n, False),
        lay(held(up_x.got, first.arrived[2]), info, 0, hidden_n, False),
        lay(down_x.got, info, 0, hidden_n, True),
    )


def solution(mesh):
    context, tensor = mesh.devices.shape
    count = context // (2 * RING)
    fine = Mesh(mesh.devices.reshape(RING, count, 2, tensor), ("a", "b", "core", "tp"))
    ctx = ("a", "b", "core")
    rows, both, turned = P(ctx, None), P(ctx, "tp"), P("tp", ctx)
    return jax.shard_map(
        functools.partial(shards, count),
        mesh=fine,
        in_specs=(rows, P(), both, both, both, P(), P(), turned, P(), both, both, turned, P(), rows),
        out_specs=(rows, rows, P(), both, both, both, P(), P(), turned, P(), both, both, turned),
        check_vma=False,
    )
```

time: 2050 us -> 542 us (0.26)
  waiting for transfers between devices: 1520 us -> 274 us
  matrix products: 240 us -> 19.2 us
  other arithmetic: 151 us -> 10.7 us
  Pallas kernels: 0 us -> 98.2 us
  starting transfers between devices: 1.74 us -> 91 us
  blocking collectives: 43.9 us -> 0 us
  local copies, waits for them, and re-layouts: 75.4 us -> 36.3 us
    reduce_scatter x3 -> x0, waiting for transfers between devices: 1060 us -> none  [the longest x1 735 us: shards(): lax.psum_scatter(jnp.concatenate([transposed_times(left_one, grad_proj),...]
    all_gather x6 -> x0, waiting for transfers between devices: 398 us -> none  [the longest x1 167 us: shards(): lax.all_gather(paired, 'ctx', axis=1, tiled=True)]
    ppermute x0 -> x120, waiting for transfers between devices: none -> 274 us  [the longest x53 194 us: ring_permute(): lax.ppermute(value, 'a', [(i, (i + step) % RING) for i in range(RING)])]
    dot_general x57 -> x20, matrix products: 240 us -> 19.2 us  [dot(): lax.dot_general(left, right, (((left_dim,), (right_dim,)), ((), ())), pre...]
    pallas_call x0 -> x28, Pallas kernels: none -> 98.2 us  [the longest x24 83.2 us: call(): pl.pallas_call(kernel, grid_spec=pltpu.PrefetchScalarGridSpec(num_scalar_...]
    concatenate x8 -> x0, other arithmetic: 94.4 us -> none  [the longest x1 63.3 us: shards(): jnp.concatenate([transposed_times(left_one, grad_proj), transposed_times(...]
    ppermute x0 -> x120, starting transfers between devices: none -> 91 us  [the longest x61 42.5 us: move(): return lax.ppermute(v, axis, [(0, 1), (1, 0)])]
    psum x3 -> x0, waiting for transfers between devices: 61 us -> none  [the longest x1 32.4 us: shards(): lax.psum(grad_second_part.astype(jnp.bfloat16), 'tp').astype(jnp.float32)]
  transfers between devices with their start and end apart: 12 -> 120, of which waited for: 11 -> 53; matrix products, arithmetic and copies ran while one was open for 14% -> 9% of each run, Pallas kernels for 0% -> 15%
where the time goes in v1:
time: 542 us; the launch traced here: 533 us
  waiting for transfers between devices  274 us (51%)
  Pallas kernels  98.2 us (18%)
  starting transfers between devices  91 us (17%)
  local copies, waits for them, and re-layouts  36.3 us (7%)
  matrix products  19.2 us (4%)
  other arithmetic  10.7 us (2%)
    ppermute x53, waiting for transfers between devices, ring_permute(): lax.ppermute(value, 'a', [(i, (i + step) % RING) for i in range(RING)])  194 us
    pallas_call x24, Pallas kernels, call(): pl.pallas_call(kernel, grid_spec=pltpu.PrefetchScalarGridSpec(num_scalar_...  83.2 us
    ppermute x61, waiting for transfers between devices, move(): return lax.ppermute(v, axis, [(0, 1), (1, 0)])  80.6 us
    ppermute x61, starting transfers between devices, move(): return lax.ppermute(v, axis, [(0, 1), (1, 0)])  42.5 us
    ppermute x53, starting transfers between devices, ring_permute(): lax.ppermute(value, 'a', [(i, (i + step) % RING) for i in range(RING)])  41.2 us
    dot_general x20, matrix products, dot(): lax.dot_general(left, right, (((left_dim,), (right_dim,)), ((), ())), pre...  19.2 us
    pallas_call x4, Pallas kernels, lay(): pl.pallas_call(functools.partial(lay_kernel, turned), grid_spec=pltpu.Pre...  15 us
    unnamed x206, local copies, waits for them, and re-layouts  13.3 us
  transfers between devices with their start and end apart: 120, of which 53 were waited for; matrix products, arithmetic and copies ran while one was open for 9% of the time, Pallas kernels for 15%

profile of v1, /device:TPU:0, one launch (start us, length us, event | category | flops | bytes accessed | tf_op | source)
XLA Modules:
  0.0 532.6 jit_solution(6117566645763609368)
XLA Ops:
  17.3 13.8 %collective-permute-done.1 = bf16[128,640]{1,0:T(8,128)(2,1)S(1)} collective-permute-done((bf16[128,640]{1,0:T(8,128)(2,1)}, bf16[128,640]{1,0:T(8,128)(2,1)S(1)}, u32[]{:S(2)}, u32[]{:S(2)}) %collective-permute-start.1) | collective-permute-done | bytes 163872 | tf_op jit(solution)/shard_map/ppermute | solution.py:57
  41.0 6.8 %collective-permute-done.3.w1.refs_4_ = bf16[512,640]{1,0:T(8,128)(2,1)S(1)} collective-permute-done((bf16[512,640]{1,0:T(8,128)(2,1)S(1)}, bf16[512,640]{1,0:T(8,128)(2,1)S(1)}, u32[]{:S(2)}, u32[]{:S(2)}) %collective-permute-start.3) | collective-permute-done | bytes 655392 | tf_op jit(solution)/shard_map/ppermute | solution.py:66
  60.1 4.9 collective-permute-done.10.mine_ref
  91.2 5.0 shard_map.243
  113.3 6.1 %collective-permute-done.24 = bf16[128,2048]{1,0:T(8,128)(2,1)S(1)} collective-permute-done((bf16[128,2048]{1,0:T(8,128)(2,1)S(1)}, bf16[128,2048]{1,0:T(8,128)(2,1)S(1)}, u32[]{:S(2)}, u32[]{:S(2)}) %collective-permute-start.24) | collective-permute-done | bytes 524320 | tf_op jit(solution)/shard_map/ppermute | solution.py:57
  119.4 8.4 %collective-permute-done.17 = bf16[96,2048]{1,0:T(8,128)(2,1)S(1)} collective-permute-done((bf16[96,2048]{1,0:T(8,128)(2,1)S(1)}, bf16[96,2048]{1,0:T(8,128)(2,1)S(1)}, u32[]{:S(2)}, u32[]{:S(2)}) %collective-permute-start.17) | collective-permute-done | bytes 393248 | tf_op jit(solution)/shard_map/ppermute | solution.py:57
  131.3 9.6 %collective-permute-done.20 = bf16[96,2048]{1,0:T(8,128)(2,1)S(1)} collective-permute-done((bf16[96,2048]{1,0:T(8,128)(2,1)S(1)}, bf16[96,2048]{1,0:T(8,128)(2,1)S(1)}, u32[]{:S(2)}, u32[]{:S(2)}) %collective-permute-start.20) | collective-permute-done | bytes 393248 | tf_op jit(solution)/shard_map/ppermute | solution.py:57
  145.8 7.3 %collective-permute-done.21 = bf16[96,2048]{1,0:T(8,128)(2,1)S(1)} collective-permute-done((bf16[96,2048]{1,0:T(8,128)(2,1)S(1)}, bf16[96,2048]{1,0:T(8,128)(2,1)S(1)}, u32[]{:S(2)}, u32[]{:S(2)}) %collective-permute-start.21) | collective-permute-done | bytes 393248 | tf_op jit(solution)/shard_map/ppermute | solution.py:57
  155.7 15.4 %collective-permute-done.27 = bf16[128,1024]{1,0:T(8,128)(2,1)S(1)} collective-permute-done((bf16[128,1024]{1,0:T(8,128)(2,1)S(1)}, bf16[128,1024]{1,0:T(8,128)(2,1)S(1)}, u32[]{:S(2)}, u32[]{:S(2)}) %collective-permute-start.27) | collective-permute-done | bytes 262176 | tf_op jit(solution)/shard_map/ppermute | solution.py:57
  172.0 9.3 %collective-permute-done.28 = bf16[128,1024]{1,0:T(8,128)(2,1)S(1)} collective-permute-done((bf16[128,1024]{1,0:T(8,128)(2,1)S(1)}, bf16[128,1024]{1,0:T(8,128)(2,1)S(1)}, u32[]{:S(2)}, u32[]{:S(2)}) %collective-permute-start.28) | collective-permute-done | bytes 262176 | tf_op jit(solution)/shard_map/ppermute | solution.py:57
  182.9 9.4 %collective-permute-done.29 = bf16[128,1024]{1,0:T(8,128)(2,1)S(1)} collective-permute-done((bf16[128,1024]{1,0:T(8,128)(2,1)S(1)}, bf16[128,1024]{1,0:T(8,128)(2,1)S(1)}, u32[]{:S(2)}, u32[]{:S(2)}) %collective-permute-start.29) | collective-permute-done | bytes 262176 | tf_op jit(solution)/shard_map/ppermute | solution.py:57
  192.4 8.3 %collective-permute-done.31.cm_ref = bf16[96,2048]{1,0:T(8,128)(2,1)S(1)} collective-permute-done((bf16[96,2048]{1,0:T(8,128)(2,1)S(1)}, bf16[96,2048]{1,0:T(8,128)(2,1)S(1)}, u32[]{:S(2)}, u32[]{:S(2)}) %collective-permute-start.31) | collective-permute-done | bytes 393248 | tf_op jit(solution)/shard_map/ppermute | solution.py:57
  210.5 7.3 %collective-permute-done.35.ho_ref = bf16[96,2048]{1,0:T(8,128)(2,1)S(1)} collective-permute-done((bf16[96,2048]{1,0:T(8,128)(2,1)S(1)}, bf16[96,2048]{1,0:T(8,128)(2,1)S(1)}, u32[]{:S(2)}, u32[]{:S(2)}) %collective-permute-start.35) | collective-permute-done | bytes 393248 | tf_op jit(solution)/shard_map/ppermute | solution.py:66
  220.1 7.0 %collective-permute-done.37.co_ref = bf16[96,2048]{1,0:T(8,128)(2,1)S(1)} collective-permute-done((bf16[96,2048]{1,0:T(8,128)(2,1)S(1)}, bf16[96,2048]{1,0:T(8,128)(2,1)S(1)}, u32[]{:S(2)}, u32[]{:S(2)}) %collective-permute-start.37) | collective-permute-done | bytes 393248 | tf_op jit(solution)/shard_map/ppermute | solution.py:66
  235.8 7.6 %collective-permute-done.47.co_ref = bf16[96,2048]{1,0:T(8,128)(2,1)S(1)} collective-permute-done((bf16[96,2048]{1,0:T(8,128)(2,1)S(1)}, bf16[96,2048]{1,0:T(8,128)(2,1)S(1)}, u32[]{:S(2)}, u32[]{:S(2)}) %collective-permute-start.47) | collective-permute-done | bytes 393248 | tf_op jit(solution)/shard_map/ppermute | solution.py:66
  243.5 7.7 %shard_map.247 = (bf16[768,3072]{1,0:T(8,128)(2,1)S(1)}, bf16[96,2048]{1,0:T(8,128)(2,1)S(1)}, bf16[96,2048]{1,0:T(8,128)(2,1)S(1)}, bf16[96,2048]{1,0:T(8,128)(2,1)S(1)}, bf16[96,2048]{1,0:T(8,128)(2,1)S(1)}) custom-call(s32[8]{0:T(128)S(1)} %concatenate.57.info_ref.refs_0_.place_ref, bf16[96,2048]{1,0:T(8,128)(2,1)S(1)} %collective-permute-done.26.hm_ref, ...), custom_call_target="tpu_custom_call" | custom-call | flops 4831838208 | bytes 15728640 | tf_op jit(solution)/shard_map/pallas_call | solution.py:553
  251.8 7.7 %shard_map.248 = (bf16[768,3072]{1,0:T(8,128)(2,1)S(1)}, bf16[96,2048]{1,0:T(8,128)(2,1)S(1)}, bf16[96,2048]{1,0:T(8,128)(2,1)S(1)}, bf16[96,2048]{1,0:T(8,128)(2,1)S(1)}, bf16[96,2048]{1,0:T(8,128)(2,1)S(1)}) custom-call(s32[8]{0:T(128)S(1)} %concatenate.57.info_ref.refs_0_.place_ref, ...), custom_call_target="tpu_custom_call", output_to_operand_aliasing={{0}: (13, {})} | custom-call | flops 4831838208 | bytes 15728640 | tf_op jit(solution)/shard_map/pallas_call | solution.py:553
  261.5 7.7 %shard_map.249 = (bf16[768,3072]{1,0:T(8,128)(2,1)S(1)}, bf16[96,2048]{1,0:T(8,128)(2,1)S(1)}, bf16[96,2048]{1,0:T(8,128)(2,1)S(1)}, bf16[96,2048]{1,0:T(8,128)(2,1)S(1)}, bf16[96,2048]{1,0:T(8,128)(2,1)S(1)}) custom-call(s32[8]{0:T(128)S(1)} %concatenate.57.info_ref.refs_0_.place_ref, ...), custom_call_target="tpu_custom_call", output_to_operand_aliasing={{0}: (13, {})} | custom-call | flops 4831838208 | bytes 15728640 | tf_op jit(solution)/shard_map/pallas_call | solution.py:553
  273.4 7.7 %shard_map.250 = (bf16[768,3072]{1,0:T(8,128)(2,1)S(1)}, bf16[96,2048]{1,0:T(8,128)(2,1)S(1)}, bf16[96,2048]{1,0:T(8,128)(2,1)S(1)}, bf16[96,2048]{1,0:T(8,128)(2,1)S(1)}, bf16[96,2048]{1,0:T(8,128)(2,1)S(1)}) custom-call(s32[8]{0:T(128)S(1)} %concatenate.57.info_ref.refs_0_.place_ref, ...), custom_call_target="tpu_custom_call", output_to_operand_aliasing={{0}: (13, {})} | custom-call | flops 4831838208 | bytes 15728640 | tf_op jit(solution)/shard_map/pallas_call | solution.py:553
  286.9 6.7 %collective-permute-done.53 = bf16[96,2048]{1,0:T(8,128)(2,1)S(1)} collective-permute-done((bf16[96,2048]{1,0:T(8,128)(2,1)S(1)}, bf16[96,2048]{1,0:T(8,128)(2,1)S(1)}, u32[]{:S(2)}, u32[]{:S(2)}) %collective-permute-start.53) | collective-permute-done | bytes 393248 | tf_op jit(solution)/shard_map/ppermute | solution.py:57
  312.5 7.8 %collective-permute-done.55.gm_ref = bf16[96,2048]{1,0:T(8,128)(2,1)S(1)} collective-permute-done((bf16[96,2048]{1,0:T(8,128)(2,1)S(1)}, bf16[96,2048]{1,0:T(8,128)(2,1)S(1)}, u32[]{:S(2)}, u32[]{:S(2)}) %collective-permute-start.55) | collective-permute-done | bytes 393248 | tf_op jit(solution)/shard_map/ppermute | solution.py:57
  325.1 7.7 %collective-permute-done.56.gm_ref = bf16[96,2048]{1,0:T(8,128)(2,1)S(1)} collective-permute-done((bf16[96,2048]{1,0:T(8,128)(2,1)S(1)}, bf16[96,2048]{1,0:T(8,128)(2,1)S(1)}, u32[]{:S(2)}, u32[]{:S(2)}) %collective-permute-start.56) | collective-permute-done | bytes 393248 | tf_op jit(solution)/shard_map/ppermute | solution.py:57
  333.6 8.4 %shard_map.252 = (bf16[192,256]{1,0:T(8,128)(2,1)S(1)}, f32[64,192]{1,0:T(8,128)S(1)}, f32[16,192,128]{2,1,0:T(8,128)S(1)}) custom-call(s32[8]{0:T(128)S(1)} %concatenate.57.info_ref.refs_0_.place_ref, bf16[96,2048]{1,0:T(8,128)(2,1)S(1)} %collective-permute-done.55.gm_ref, ...), custom_call_target="tpu_custom_call", output_to_operand_aliasing={{2}: (15, {})} | custom-call | flops 3019898880 | bytes 6291456 | tf_op jit(solution)/shard_map/pallas_call | solution.py:553
  347.3 6.3 %shard_map.253 = (bf16[192,256]{1,0:T(8,128)(2,1)S(1)}, f32[64,192]{1,0:T(8,128)S(1)}, f32[16,192,128]{2,1,0:T(8,128)S(1)}) custom-call(s32[8]{0:T(128)S(1)} %concatenate.57.info_ref.refs_0_.place_ref, bf16[96,2048]{1,0:T(8,128)(2,1)S(1)} %collective-permute-done.56.gm_ref, ...), custom_call_target="tpu_custom_call", output_to_operand_aliasing={{2}: (15, {})} | custom-call | flops 3019898880 | bytes 6291456 | tf_op jit(solution)/shard_map/pallas_call | solution.py:553
  361.7 9.1 %collective-permute-done.70 = bf16[512,1024]{1,0:T(8,128)(2,1)} collective-permute-done((bf16[512,1024]{1,0:T(8,128)(2,1)S(1)}, bf16[512,1024]{1,0:T(8,128)(2,1)}, u32[]{:S(2)}, u32[]{:S(2)}) %collective-permute-start.70) | collective-permute-done | bytes 1048608 | tf_op jit(solution)/shard_map/ppermute | solution.py:66
  376.6 8.2 %collective-permute-done.74.refs_1_ = bf16[128,1024]{1,0:T(8,128)(2,1)S(1)} collective-permute-done((bf16[128,1024]{1,0:T(8,128)(2,1)S(1)}, bf16[128,1024]{1,0:T(8,128)(2,1)S(1)}, u32[]{:S(2)}, u32[]{:S(2)}) %collective-permute-start.74) | collective-permute-done | bytes 262176 | tf_op jit(solution)/shard_map/ppermute | solution.py:57
  403.1 6.7 %collective-permute-done.76 = bf16[96,2048]{1,0:T(8,128)(2,1)S(1)} collective-permute-done((bf16[96,2048]{1,0:T(8,128)(2,1)S(1)}, bf16[96,2048]{1,0:T(8,128)(2,1)S(1)}, u32[]{:S(2)}, u32[]{:S(2)}) %collective-permute-start.76) | collective-permute-done | bytes 393248 | tf_op jit(solution)/shard_map/ppermute | solution.py:57
  410.0 9.6 %collective-permute-done.80.refs_2_ = bf16[128,1024]{1,0:T(8,128)(2,1)S(1)} collective-permute-done((bf16[128,1024]{1,0:T(8,128)(2,1)S(1)}, bf16[128,1024]{1,0:T(8,128)(2,1)S(1)}, u32[]{:S(2)}, u32[]{:S(2)}) %collective-permute-start.80) | collective-permute-done | bytes 262176 | tf_op jit(solution)/shard_map/ppermute | solution.py:57
  422.9 8.3 %collective-permute-done.81 = bf16[96,2048]{1,0:T(8,128)(2,1)S(1)} collective-permute-done((bf16[96,2048]{1,0:T(8,128)(2,1)S(1)}, bf16[96,2048]{1,0:T(8,128)(2,1)S(1)}, u32[]{:S(2)}, u32[]{:S(2)}) %collective-permute-start.81) | collective-permute-done | bytes 393248 | tf_op jit(solution)/shard_map/ppermute | solution.py:57
  445.2 5.1 collective-permute-done.88
  457.0 6.7 %collective-permute-done.89 = bf16[96,2048]{1,0:T(8,128)(2,1)S(1)} collective-permute-done((bf16[96,2048]{1,0:T(8,128)(2,1)S(1)}, bf16[96,2048]{1,0:T(8,128)(2,1)S(1)}, u32[]{:S(2)}, u32[]{:S(2)}) %collective-permute-start.89) | collective-permute-done | bytes 393248 | tf_op jit(solution)/shard_map/ppermute | solution.py:66
  471.4 5.7 %collective-permute-done.94 = bf16[96,2048]{1,0:T(8,128)(2,1)S(1)} collective-permute-done((bf16[96,2048]{1,0:T(8,128)(2,1)S(1)}, bf16[96,2048]{1,0:T(8,128)(2,1)S(1)}, u32[]{:S(2)}, u32[]{:S(2)}) %collective-permute-start.94) | collective-permute-done | bytes 393248 | tf_op jit(solution)/shard_map/ppermute | solution.py:57
  (565 shorter events, 276.3 us)
Async XLA Ops:
  11.6 22.5 %collective-permute-start.6 = (bf16[96,2048]{1,0:T(8,128)(2,1)S(1)}, bf16[96,2048]{1,0:T(8,128)(2,1)}, u32[]{:S(2)}, u32[]{:S(2)}) collective-permute-start(bf16[96,2048]{1,0:T(8,128)(2,1)S(1)} %get-tuple-element.401.mine_ref), channel_id=1, source_target_pairs={{0,8},{8,16},{16,24},{24,0},{1,9},{9,17},{17,25},{25,1},{2,10},{10... | collective-permute-start | bytes 1179656 | tf_op jit(solution)/shard_map/ppermute | solution.py:57
  13.2 18.0 %collective-permute-start.1 = (bf16[128,640]{1,0:T(8,128)(2,1)}, bf16[128,640]{1,0:T(8,128)(2,1)S(1)}, u32[]{:S(2)}, u32[]{:S(2)}) collective-permute-start(bf16[128,640]{1,0:T(8,128)(2,1)} %get-tuple-element.472), channel_id=1, source_target_pairs={{0,16},{8,24},{16,0},{24,8},{1,17},{9,25},{17,1},{25,9},{2,18},{10... | collective-permute-start | bytes 491528 | tf_op jit(solution)/shard_map/ppermute | solution.py:57
  14.2 17.0 %collective-permute-start.2 = (bf16[128,640]{1,0:T(8,128)(2,1)S(1)}, bf16[128,640]{1,0:T(8,128)(2,1)S(1)}, u32[]{:S(2)}, u32[]{:S(2)}) collective-permute-start(bf16[128,640]{1,0:T(8,128)(2,1)S(1)} %get-tuple-element.471), channel_id=1, source_target_pairs={{0,24},{8,0},{16,8},{24,16},{1,25},{9,1},{17,9},{25,17},{2,26},{10... | collective-permute-start | bytes 491528 | tf_op jit(solution)/shard_map/ppermute | solution.py:57
  34.1 31.7 %collective-permute-start.4 = (bf16[512,640]{1,0:T(8,128)(2,1)S(1)}, bf16[512,640]{1,0:T(8,128)(2,1)S(1)}, u32[]{:S(2)}, u32[]{:S(2)}) collective-permute-start(bf16[512,640]{1,0:T(8,128)(2,1)S(1)} %bitcast.203), channel_id=1, source_target_pairs={{0,2},{2,0},{1,3},{3,1},{4,6},{6,4},{5,7},{7,5},{8,10},{10,8},{9,1... | collective-permute-start | bytes 1966088 | tf_op jit(solution)/shard_map/ppermute | solution.py:66
  47.8 18.0 %collective-permute-start.5 = (bf16[512,640]{1,0:T(8,128)(2,1)S(1)}, bf16[512,640]{1,0:T(8,128)(2,1)S(1)}, u32[]{:S(2)}, u32[]{:S(2)}) collective-permute-start(bf16[512,640]{1,0:T(8,128)(2,1)S(1)} %collective-permute-done.3.w1.refs_4_), channel_id=1, source_target_pairs={{0,2},{2,0},{1,3},{3,1},{4,6},{6,4},{5,7},{7,5},{8,10},{10,8},{9,1... | collective-permute-start | bytes 1966088 | tf_op jit(solution)/shard_map/ppermute | solution.py:66
  55.2 22.1 %collective-permute-start.12 = (bf16[128,2048]{1,0:T(8,128)(2,1)S(1)}, bf16[128,2048]{1,0:T(8,128)(2,1)S(1)}, u32[]{:S(2)}, u32[]{:S(2)}) collective-permute-start(bf16[128,2048]{1,0:T(8,128)(2,1)S(1)} %get-tuple-element.236), channel_id=1, source_target_pairs={{0,8},{8,16},{16,24},{24,0},{1,9},{9,17},{17,25},{25,1},{2,10},{10... | collective-permute-start | bytes 1572872 | tf_op jit(solution)/shard_map/ppermute | solution.py:57
  65.5 20.7 %collective-permute-start.22 = (bf16[128,2048]{1,0:T(8,128)(2,1)}, bf16[128,2048]{1,0:T(8,128)(2,1)}, u32[]{:S(2)}, u32[]{:S(2)}) collective-permute-start(bf16[128,2048]{1,0:T(8,128)(2,1)} %get-tuple-element.261), channel_id=1, source_target_pairs={{0,24},{8,0},{16,8},{24,16},{1,25},{9,1},{17,9},{25,17},{2,26},{10... | collective-permute-start | bytes 1572872 | tf_op jit(solution)/shard_map/ppermute | solution.py:57
  107.6 20.2 %collective-permute-start.17 = (bf16[96,2048]{1,0:T(8,128)(2,1)S(1)}, bf16[96,2048]{1,0:T(8,128)(2,1)S(1)}, u32[]{:S(2)}, u32[]{:S(2)}) collective-permute-start(bf16[96,2048]{1,0:T(8,128)(2,1)S(1)} %add_convert_fusion.19), channel_id=1, source_target_pairs={{0,8},{8,16},{16,24},{24,0},{1,9},{9,17},{17,25},{25,1},{2,10},{10... | collective-permute-start | bytes 1179656 | tf_op jit(solution)/shard_map/ppermute | solution.py:57
  107.7 20.1 %collective-permute-start.16 = (bf16[96,2048]{1,0:T(8,128)(2,1)S(1)}, bf16[96,2048]{1,0:T(8,128)(2,1)S(1)}, u32[]{:S(2)}, u32[]{:S(2)}) collective-permute-start(bf16[96,2048]{1,0:T(8,128)(2,1)S(1)} %get-tuple-element.243), channel_id=1, source_target_pairs={{0,1},{1,0},{2,3},{3,2},{4,5},{5,4},{6,7},{7,6},{8,9},{9,8},{10,11... | collective-permute-start | bytes 1179656 | tf_op jit(solution)/shard_map/ppermute | solution.py:66
  119.4 35.9 %collective-permute-start.25 = (bf16[128,1024]{1,0:T(8,128)(2,1)S(1)}, bf16[128,1024]{1,0:T(8,128)(2,1)S(1)}, u32[]{:S(2)}, u32[]{:S(2)}) collective-permute-start(bf16[128,1024]{1,0:T(8,128)(2,1)S(1)} %get-tuple-element.263), channel_id=1, source_target_pairs={{0,8},{8,16},{16,24},{24,0},{1,9},{9,17},{17,25},{25,1},{2,10},{10... | collective-permute-start | bytes 786440 | tf_op jit(solution)/shard_map/ppermute | solution.py:57
  143.2 57.7 %collective-permute-start.38 = (bf16[512,2048]{1,0:T(8,128)(2,1)S(1)}, bf16[512,2048]{1,0:T(8,128)(2,1)S(1)}, u32[]{:S(2)}, u32[]{:S(2)}) collective-permute-start(bf16[512,2048]{1,0:T(8,128)(2,1)S(1)} %bitcast.220), channel_id=1, source_target_pairs={{0,4},{4,0},{1,5},{5,1},{2,6},{6,2},{3,7},{7,3},{8,12},{12,8},{9,1... | collective-permute-start | bytes 6291464 | tf_op jit(solution)/shard_map/ppermute | solution.py:66
  153.4 17.7 %collective-permute-start.27 = (bf16[128,1024]{1,0:T(8,128)(2,1)S(1)}, bf16[128,1024]{1,0:T(8,128)(2,1)S(1)}, u32[]{:S(2)}, u32[]{:S(2)}) collective-permute-start(bf16[128,1024]{1,0:T(8,128)(2,1)S(1)} %get-tuple-element.265), channel_id=1, source_target_pairs={{0,24},{8,0},{16,8},{24,16},{1,25},{9,1},{17,9},{25,17},{2,26},{10... | collective-permute-start | bytes 786440 | tf_op jit(solution)/shard_map/ppermute | solution.py:57
  155.3 16.7 %collective-permute-start.26 = (bf16[96,2048]{1,0:T(8,128)(2,1)S(1)}, bf16[96,2048]{1,0:T(8,128)(2,1)S(1)}, u32[]{:S(2)}, u32[]{:S(2)}) collective-permute-start(bf16[96,2048]{1,0:T(8,128)(2,1)S(1)} %multiply_convert_fusion.hm_ref), channel_id=1, source_target_pairs={{0,8},{8,16},{16,24},{24,0},{1,9},{9,17},{17,25},{25,1},{2,10},{10... | collective-permute-start | bytes 1179656 | tf_op jit(solution)/shard_map/ppermute | solution.py:57
  171.9 71.6 %collective-permute-start.39 = (bf16[512,2048]{1,0:T(8,128)(2,1)S(1)}, bf16[512,2048]{1,0:T(8,128)(2,1)S(1)}, u32[]{:S(2)}, u32[]{:S(2)}) collective-permute-start(bf16[512,2048]{1,0:T(8,128)(2,1)S(1)} %bitcast.221), channel_id=1, source_target_pairs={{0,2},{2,0},{1,3},{3,1},{4,6},{6,4},{5,7},{7,5},{8,10},{10,8},{9,1... | collective-permute-start | bytes 6291464 | tf_op jit(solution)/shard_map/ppermute | solution.py:66
  182.8 17.9 %collective-permute-start.31 = (bf16[96,2048]{1,0:T(8,128)(2,1)S(1)}, bf16[96,2048]{1,0:T(8,128)(2,1)S(1)}, u32[]{:S(2)}, u32[]{:S(2)}) collective-permute-start(bf16[96,2048]{1,0:T(8,128)(2,1)S(1)} %get-tuple-element.270.cm_ref), channel_id=1, source_target_pairs={{0,8},{8,16},{16,24},{24,0},{1,9},{9,17},{17,25},{25,1},{2,10},{10... | collective-permute-start | bytes 1179656 | tf_op jit(solution)/shard_map/ppermute | solution.py:57
  200.9 29.8 %collective-permute-start.41 = (bf16[512,1024]{1,0:T(8,128)(2,1)S(1)}, bf16[512,1024]{1,0:T(8,128)(2,1)S(1)}, u32[]{:S(2)}, u32[]{:S(2)}) collective-permute-start(bf16[512,1024]{1,0:T(8,128)(2,1)S(1)} %bitcast.226), channel_id=1, source_target_pairs={{0,4},{4,0},{1,5},{5,1},{2,6},{6,2},{3,7},{7,3},{8,12},{12,8},{9,1... | collective-permute-start | bytes 3145736 | tf_op jit(solution)/shard_map/ppermute | solution.py:66
  205.9 37.6 %collective-permute-start.40 = (bf16[512,2048]{1,0:T(8,128)(2,1)S(1)}, bf16[512,2048]{1,0:T(8,128)(2,1)S(1)}, u32[]{:S(2)}, u32[]{:S(2)}) collective-permute-start(bf16[512,2048]{1,0:T(8,128)(2,1)S(1)} %collective-permute-done.38.p1), channel_id=1, source_target_pairs={{0,2},{2,0},{1,3},{3,1},{4,6},{6,4},{5,7},{7,5},{8,10},{10,8},{9,1... | collective-permute-start | bytes 6291464 | tf_op jit(solution)/shard_map/ppermute | solution.py:66
  284.9 22.1 %collective-permute-start.67 = (bf16[512,1024]{1,0:T(8,128)(2,1)S(1)}, bf16[512,1024]{1,0:T(8,128)(2,1)S(1)}, u32[]{:S(2)}, u32[]{:S(2)}) collective-permute-start(bf16[512,1024]{1,0:T(8,128)(2,1)S(1)} %convolution_convert_fusion.4), channel_id=1, source_target_pairs={{0,2},{2,0},{1,3},{3,1},{4,6},{6,4},{5,7},{7,5},{8,10},{10,8},{9,1... | collective-permute-start | bytes 3145736 | tf_op jit(solution)/shard_map/ppermute | solution.py:66
  299.8 60.4 %collective-permute-start.66 = (bf16[512,1024]{1,0:T(8,128)(2,1)S(1)}, bf16[512,1024]{1,0:T(8,128)(2,1)S(1)}, u32[]{:S(2)}, u32[]{:S(2)}) collective-permute-start(bf16[512,1024]{1,0:T(8,128)(2,1)S(1)} %convolution_convert_fusion.5), channel_id=1, source_target_pairs={{0,2},{2,0},{1,3},{3,1},{4,6},{6,4},{5,7},{7,5},{8,10},{10,8},{9,1... | collective-permute-start | bytes 3145736 | tf_op jit(solution)/shard_map/ppermute | solution.py:66
  303.4 41.9 %collective-permute-start.71 = (bf16[512,1024]{1,0:T(8,128)(2,1)S(1)}, bf16[512,1024]{1,0:T(8,128)(2,1)S(1)}, u32[]{:S(2)}, u32[]{:S(2)}) collective-permute-start(bf16[512,1024]{1,0:T(8,128)(2,1)S(1)} %convolution_convert_fusion.2), channel_id=1, source_target_pairs={{0,2},{2,0},{1,3},{3,1},{4,6},{6,4},{5,7},{7,5},{8,10},{10,8},{9,1... | collective-permute-start | bytes 3145736 | tf_op jit(solution)/shard_map/ppermute | solution.py:66
  311.3 34.0 %collective-permute-start.69 = (bf16[512,1024]{1,0:T(8,128)(2,1)}, bf16[512,1024]{1,0:T(8,128)(2,1)S(1)}, u32[]{:S(2)}, u32[]{:S(2)}) collective-permute-start(bf16[512,1024]{1,0:T(8,128)(2,1)} %add_convert_fusion.4), channel_id=1, source_target_pairs={{0,4},{4,0},{1,5},{5,1},{2,6},{6,2},{3,7},{7,3},{8,12},{12,8},{9,1... | collective-permute-start | bytes 3145736 | tf_op jit(solution)/shard_map/ppermute | solution.py:66
  344.5 75.8 %collective-permute-start.108 = (bf16[512,1024]{1,0:T(8,128)(2,1)S(1)}, bf16[512,1024]{1,0:T(8,128)(2,1)S(1)}, u32[]{:S(2)}, u32[]{:S(2)}) collective-permute-start(bf16[512,1024]{1,0:T(8,128)(2,1)S(1)} %convolution_convert_fusion), channel_id=1, source_target_pairs={{0,2},{2,0},{1,3},{3,1},{4,6},{6,4},{5,7},{7,5},{8,10},{10,8},{9,1... | collective-permute-start | bytes 3145736 | tf_op jit(solution)/shard_map/ppermute | solution.py:66
  345.3 25.5 %collective-permute-start.70 = (bf16[512,1024]{1,0:T(8,128)(2,1)S(1)}, bf16[512,1024]{1,0:T(8,128)(2,1)}, u32[]{:S(2)}, u32[]{:S(2)}) collective-permute-start(bf16[512,1024]{1,0:T(8,128)(2,1)S(1)} %add_convert_fusion.5), channel_id=1, source_target_pairs={{0,4},{4,0},{1,5},{5,1},{2,6},{6,2},{3,7},{7,3},{8,12},{12,8},{9,1... | collective-permute-start | bytes 3145736 | tf_op jit(solution)/shard_map/ppermute | solution.py:66
  357.7 16.7 %collective-permute-start.77 = (bf16[128,1024]{1,0:T(8,128)(2,1)S(1)}, bf16[128,1024]{1,0:T(8,128)(2,1)S(1)}, u32[]{:S(2)}, u32[]{:S(2)}) collective-permute-start(bf16[128,1024]{1,0:T(8,128)(2,1)S(1)} %get-tuple-element.331), channel_id=1, source_target_pairs={{0,24},{8,0},{16,8},{24,16},{1,25},{9,1},{17,9},{25,17},{2,26},{10... | collective-permute-start | bytes 786440 | tf_op jit(solution)/shard_map/ppermute | solution.py:57
  376.3 43.2 %collective-permute-start.84 = (bf16[512,1024]{1,0:T(8,128)(2,1)S(1)}, bf16[512,1024]{1,0:T(8,128)(2,1)S(1)}, u32[]{:S(2)}, u32[]{:S(2)}) collective-permute-start(bf16[512,1024]{1,0:T(8,128)(2,1)S(1)} %add_convert_fusion.1), channel_id=1, source_target_pairs={{0,4},{4,0},{1,5},{5,1},{2,6},{6,2},{3,7},{7,3},{8,12},{12,8},{9,1... | collective-permute-start | bytes 3145736 | tf_op jit(solution)/shard_map/ppermute | solution.py:66
  401.0 64.5 %collective-permute-start.116 = (bf16[512,256]{1,0:T(8,128)(2,1)S(1)}, bf16[512,256]{1,0:T(8,128)(2,1)S(1)}, u32[]{:S(2)}, u32[]{:S(2)}) collective-permute-start(bf16[512,256]{1,0:T(8,128)(2,1)S(1)} %convolution_convert_fusion.8), channel_id=1, source_target_pairs={{0,2},{2,0},{1,3},{3,1},{4,6},{6,4},{5,7},{7,5},{8,10},{10,8},{9,1... | collective-permute-start | bytes 786440 | tf_op jit(solution)/shard_map/ppermute | solution.py:66
  401.8 31.1 %collective-permute-start.65 = (bf16[96,2048]{1,0:T(8,128)(2,1)S(1)}, bf16[96,2048]{1,0:T(8,128)(2,1)S(1)}, u32[]{:S(2)}, u32[]{:S(2)}) collective-permute-start(bf16[96,2048]{1,0:T(8,128)(2,1)S(1)} %get-tuple-element.319), channel_id=1, source_target_pairs={{0,1},{1,0},{2,3},{3,2},{4,5},{5,4},{6,7},{7,6},{8,9},{9,8},{10,11... | collective-permute-start | bytes 1179656 | tf_op jit(solution)/shard_map/ppermute | solution.py:66
  431.3 22.8 %collective-permute-start.82 = (bf16[96,2048]{1,0:T(8,128)(2,1)S(1)}, bf16[96,2048]{1,0:T(8,128)(2,1)S(1)}, u32[]{:S(2)}, u32[]{:S(2)}) collective-permute-start(bf16[96,2048]{1,0:T(8,128)(2,1)S(1)} %add_convert_fusion.11), channel_id=1, source_target_pairs={{0,8},{8,16},{16,24},{24,0},{1,9},{9,17},{17,25},{25,1},{2,10},{10... | collective-permute-start | bytes 1179656 | tf_op jit(solution)/shard_map/ppermute | solution.py:57
  480.1 20.3 %collective-permute-start.110 = (bf16[128,1024]{1,0:T(8,128)(2,1)}, bf16[128,1024]{1,0:T(8,128)(2,1)}, u32[]{:S(2)}, u32[]{:S(2)}) collective-permute-start(bf16[128,1024]{1,0:T(8,128)(2,1)} %get-tuple-element.413), channel_id=1, source_target_pairs={{0,8},{8,16},{16,24},{24,0},{1,9},{9,17},{17,25},{25,1},{2,10},{10... | collective-permute-start | bytes 786440 | tf_op jit(solution)/shard_map/ppermute | solution.py:57
  483.6 18.0 %collective-permute-start.111 = (bf16[128,1024]{1,0:T(8,128)(2,1)S(1)}, bf16[128,1024]{1,0:T(8,128)(2,1)}, u32[]{:S(2)}, u32[]{:S(2)}) collective-permute-start(bf16[128,1024]{1,0:T(8,128)(2,1)S(1)} %copy-done.66), channel_id=1, source_target_pairs={{0,24},{8,0},{16,8},{24,16},{1,25},{9,1},{17,9},{25,17},{2,26},{10... | collective-permute-start | bytes 786440 | tf_op jit(solution)/shard_map/ppermute | solution.py:57
  500.4 18.0 %collective-permute-start.91 = (bf16[96,2048]{1,0:T(8,128)(2,1)S(1)}, bf16[96,2048]{1,0:T(8,128)(2,1)S(1)}, u32[]{:S(2)}, u32[]{:S(2)}) collective-permute-start(bf16[96,2048]{1,0:T(8,128)(2,1)S(1)} %add_convert_fusion.10.own_ref), channel_id=1, source_target_pairs={{0,1},{1,0},{2,3},{3,2},{4,5},{5,4},{6,7},{7,6},{8,9},{9,8},{10,11... | collective-permute-start | bytes 1179656 | tf_op jit(solution)/shard_map/ppermute | solution.py:66
  511.3 17.0 %collective-permute-start.113 = (bf16[128,384]{1,0:T(8,128)(2,1)S(1)}, bf16[128,384]{1,0:T(8,128)(2,1)S(1)}, u32[]{:S(2)}, u32[]{:S(2)}) collective-permute-start(bf16[128,384]{1,0:T(8,128)(2,1)S(1)} %copy-done.76), channel_id=1, source_target_pairs={{0,8},{8,16},{16,24},{24,0},{1,9},{9,17},{17,25},{25,1},{2,10},{10... | collective-permute-start | bytes 294920 | tf_op jit(solution)/shard_map/ppermute | solution.py:57
  (174 other events, 2150.5 us)

commit v2 on v1

--- a/solution.py
+++ b/solution.py
@@ -15,7 +15,7 @@
 ORDER = (1, 2, 3, 0)
 LOG2E = 1.4426950408889634
 NEG = -1e30
-PAIR = 2
+PAIR = 4
 DEPTH = {"a": 2, "b": 1, "tp": 1}
 bf16 = jnp.bfloat16
 f32 = jnp.float32
@@ -147,8 +147,10 @@
     def ring(self, *due):
         self.mine.append(ring_shift(after(self.mine[-1], *due) if due else self.mine[-1], 1))
 
-    def cross(self):
-        self.other.append(swap(self.mine[len(self.other)], "tp"))
+    def cross(self, k=None):
+        k = len(self.other) if k is None else k
+        self.other += [None] * (k + 1 - len(self.other))
+        self.other[k] = swap(self.mine[k], "tp")
 
     def all(self):
         for _ in range(1, RING):
@@ -639,7 +641,7 @@
     rows_one = RowGather(h1_own, h1_other)
     rows_one.ring()
     first_step = rows_one.mine[1]
-    side_near = beside(at.assembled(side_got))
+    side_near = beside(at.assembled([side_got[0], *after_all(side_got[1:], first_step)]))
     rows_one.cross()
     rows_one.ring()
     side_w = quarters(side_near)
@@ -722,7 +724,7 @@
     h2, cot = rows_two.chunks(), rows_cot.chunks()
     feed_w = quarters(pair_near) + quarters(down_near)
 
-    step = min(512, hidden_n)
+    step = min(1024, hidden_n)
     offsets = at.offsets(width)
 
     def tokens(parts):
@@ -788,7 +790,10 @@
     grad_middle = cot_own.astype(f32) + norm_back(grad_second, gain_two, unit_two, scale_two)
     gain_two_term = jnp.sum(grad_second * unit_two, axis=0)
     rows_att = RowGather(grad_middle.astype(bf16))
-    rows_att.all()
+    for n in range(1, RING):
+        rows_att.ring(*((), events[0], events[1])[n - 1])
+        rows_att.cross()
+    rows_att.cross()
     grad_att = rows_att.chunks()
     up_own = over_b(*sums[1])
     down_own = over_b(*sums[2])

time: 542 us -> 532 us (0.982)
  waiting for transfers between devices: 274 us -> 238 us
  starting transfers between devices: 91 us -> 119 us
    ppermute x61, starting transfers between devices: 42.5 us -> 62.7 us  [move(): return lax.ppermute(v, axis, [(0, 1), (1, 0)])]
    ppermute x53, waiting for transfers between devices: 194 us -> 175 us  [ring_permute(): lax.ppermute(value, 'a', [(i, (i + step) % RING) for i in range(RING)])]
    ppermute x61, waiting for transfers between devices: 80.6 us -> 63 us  [move(): return lax.ppermute(v, axis, [(0, 1), (1, 0)])]
    ppermute x53, starting transfers between devices: 41.2 us -> 49.3 us  [ring_permute(): lax.ppermute(value, 'a', [(i, (i + step) % RING) for i in range(RING)])]
  transfers between devices with their start and end apart: 120 -> 120, of which waited for: 53 -> 53; matrix products, arithmetic and copies ran while one was open for 9% -> 10% of each run, Pallas kernels for 15% -> 16%
where the time goes in v2:
time: 532 us; the launch traced here: 524 us
  waiting for transfers between devices  238 us (45%)
  starting transfers between devices  119 us (22%)
  Pallas kernels  98.4 us (18%)
  local copies, waits for them, and re-layouts  36.3 us (7%)
  matrix products  17.3 us (3%)
  other arithmetic  10.7 us (2%)
    ppermute x53, waiting for transfers between devices, ring_permute(): lax.ppermute(value, 'a', [(i, (i + step) % RING) for i in range(RING)])  175 us
    pallas_call x24, Pallas kernels, call(): pl.pallas_call(kernel, grid_spec=pltpu.PrefetchScalarGridSpec(num_scalar_...  83.4 us
    ppermute x61, waiting for transfers between devices, move(): return lax.ppermute(v, axis, [(0, 1), (1, 0)])  63 us
    ppermute x61, starting transfers between devices, move(): return lax.ppermute(v, axis, [(0, 1), (1, 0)])  62.7 us
    ppermute x53, starting transfers between devices, ring_permute(): lax.ppermute(value, 'a', [(i, (i + step) % RING) for i in range(RING)])  49.3 us
    dot_general x20, matrix products, dot(): lax.dot_general(left, right, (((left_dim,), (right_dim,)), ((), ())), pre...  17.3 us
    pallas_call x4, Pallas kernels, lay(): pl.pallas_call(functools.partial(lay_kernel, turned), grid_spec=pltpu.Pre...  15 us
    unnamed x206, local copies, waits for them, and re-layouts  13.5 us
  transfers between devices with their start and end apart: 120, of which 53 were waited for; matrix products, arithmetic and copies ran while one was open for 10% of the time, Pallas kernels for 16%

profile of v2, /device:TPU:0, one launch (start us, length us, event | category | flops | bytes accessed | tf_op | source)
XLA Modules:
  0.0 523.8 jit_solution(8563908355767681336)
XLA Ops:
  19.0 5.4 %collective-permute-done = bf16[128,640]{1,0:T(8,128)(2,1)S(1)} collective-permute-done((bf16[128,640]{1,0:T(8,128)(2,1)S(1)}, bf16[128,640]{1,0:T(8,128)(2,1)S(1)}, u32[]{:S(2)}, u32[]{:S(2)}) %collective-permute-start) | collective-permute-done | bytes 163872 | tf_op jit(solution)/shard_map/ppermute | solution.py:57
  24.4 6.2 %collective-permute-done.1 = bf16[128,640]{1,0:T(8,128)(2,1)S(1)} collective-permute-done((bf16[128,640]{1,0:T(8,128)(2,1)S(1)}, bf16[128,640]{1,0:T(8,128)(2,1)S(1)}, u32[]{:S(2)}, u32[]{:S(2)}) %collective-permute-start.1) | collective-permute-done | bytes 163872 | tf_op jit(solution)/shard_map/ppermute | solution.py:57
  40.4 6.8 %collective-permute-done.4.w1.refs_4_ = bf16[512,640]{1,0:T(8,128)(2,1)S(1)} collective-permute-done((bf16[512,640]{1,0:T(8,128)(2,1)S(1)}, bf16[512,640]{1,0:T(8,128)(2,1)S(1)}, u32[]{:S(2)}, u32[]{:S(2)}) %collective-permute-start.4) | collective-permute-done | bytes 655392 | tf_op jit(solution)/shard_map/ppermute | solution.py:66
  59.5 5.0 collective-permute-done.10.mine_ref
  96.6 4.9 collective-permute-done.23
  112.5 5.7 %collective-permute-done.24 = bf16[128,2048]{1,0:T(8,128)(2,1)S(1)} collective-permute-done((bf16[128,2048]{1,0:T(8,128)(2,1)S(1)}, bf16[128,2048]{1,0:T(8,128)(2,1)S(1)}, u32[]{:S(2)}, u32[]{:S(2)}) %collective-permute-start.24) | collective-permute-done | bytes 524320 | tf_op jit(solution)/shard_map/ppermute | solution.py:57
  118.2 8.4 %collective-permute-done.17 = bf16[96,2048]{1,0:T(8,128)(2,1)S(1)} collective-permute-done((bf16[96,2048]{1,0:T(8,128)(2,1)S(1)}, bf16[96,2048]{1,0:T(8,128)(2,1)S(1)}, u32[]{:S(2)}, u32[]{:S(2)}) %collective-permute-start.17) | collective-permute-done | bytes 393248 | tf_op jit(solution)/shard_map/ppermute | solution.py:57
  130.7 8.7 %collective-permute-done.20 = bf16[96,2048]{1,0:T(8,128)(2,1)S(1)} collective-permute-done((bf16[96,2048]{1,0:T(8,128)(2,1)S(1)}, bf16[96,2048]{1,0:T(8,128)(2,1)S(1)}, u32[]{:S(2)}, u32[]{:S(2)}) %collective-permute-start.20) | collective-permute-done | bytes 393248 | tf_op jit(solution)/shard_map/ppermute | solution.py:57
  143.8 7.5 %collective-permute-done.21 = bf16[96,2048]{1,0:T(8,128)(2,1)S(1)} collective-permute-done((bf16[96,2048]{1,0:T(8,128)(2,1)S(1)}, bf16[96,2048]{1,0:T(8,128)(2,1)S(1)}, u32[]{:S(2)}, u32[]{:S(2)}) %collective-permute-start.21) | collective-permute-done | bytes 393248 | tf_op jit(solution)/shard_map/ppermute | solution.py:57
  155.5 13.8 %collective-permute-done.27 = bf16[128,1024]{1,0:T(8,128)(2,1)S(1)} collective-permute-done((bf16[128,1024]{1,0:T(8,128)(2,1)S(1)}, bf16[128,1024]{1,0:T(8,128)(2,1)S(1)}, u32[]{:S(2)}, u32[]{:S(2)}) %collective-permute-start.27) | collective-permute-done | bytes 262176 | tf_op jit(solution)/shard_map/ppermute | solution.py:57
  169.5 10.8 %collective-permute-done.28 = bf16[128,1024]{1,0:T(8,128)(2,1)S(1)} collective-permute-done((bf16[128,1024]{1,0:T(8,128)(2,1)S(1)}, bf16[128,1024]{1,0:T(8,128)(2,1)S(1)}, u32[]{:S(2)}, u32[]{:S(2)}) %collective-permute-start.28) | collective-permute-done | bytes 262176 | tf_op jit(solution)/shard_map/ppermute | solution.py:57
  182.0 9.3 %collective-permute-done.29 = bf16[128,1024]{1,0:T(8,128)(2,1)S(1)} collective-permute-done((bf16[128,1024]{1,0:T(8,128)(2,1)S(1)}, bf16[128,1024]{1,0:T(8,128)(2,1)S(1)}, u32[]{:S(2)}, u32[]{:S(2)}) %collective-permute-start.29) | collective-permute-done | bytes 262176 | tf_op jit(solution)/shard_map/ppermute | solution.py:57
  191.4 8.3 %collective-permute-done.31.cm_ref = bf16[96,2048]{1,0:T(8,128)(2,1)S(1)} collective-permute-done((bf16[96,2048]{1,0:T(8,128)(2,1)S(1)}, bf16[96,2048]{1,0:T(8,128)(2,1)S(1)}, u32[]{:S(2)}, u32[]{:S(2)}) %collective-permute-start.31) | collective-permute-done | bytes 393248 | tf_op jit(solution)/shard_map/ppermute | solution.py:57
  210.8 6.0 %collective-permute-done.35.ho_ref = bf16[96,2048]{1,0:T(8,128)(2,1)S(1)} collective-permute-done((bf16[96,2048]{1,0:T(8,128)(2,1)S(1)}, bf16[96,2048]{1,0:T(8,128)(2,1)S(1)}, u32[]{:S(2)}, u32[]{:S(2)}) %collective-permute-start.35) | collective-permute-done | bytes 393248 | tf_op jit(solution)/shard_map/ppermute | solution.py:66
  236.7 5.9 %collective-permute-done.47.co_ref = bf16[96,2048]{1,0:T(8,128)(2,1)S(1)} collective-permute-done((bf16[96,2048]{1,0:T(8,128)(2,1)S(1)}, bf16[96,2048]{1,0:T(8,128)(2,1)S(1)}, u32[]{:S(2)}, u32[]{:S(2)}) %collective-permute-start.47) | collective-permute-done | bytes 393248 | tf_op jit(solution)/shard_map/ppermute | solution.py:66
  242.7 7.2 %shard_map.247 = (bf16[768,3072]{1,0:T(8,128)(2,1)S(1)}, bf16[96,2048]{1,0:T(8,128)(2,1)S(1)}, bf16[96,2048]{1,0:T(8,128)(2,1)S(1)}, bf16[96,2048]{1,0:T(8,128)(2,1)S(1)}, bf16[96,2048]{1,0:T(8,128)(2,1)S(1)}) custom-call(s32[8]{0:T(128)S(1)} %concatenate.57.info_ref.refs_0_.place_ref, bf16[96,2048]{1,0:T(8,128)(2,1)S(1)} %collective-permute-done.26.hm_ref, ...), custom_call_target="tpu_custom_call" | custom-call | flops 4831838208 | bytes 15728640 | tf_op jit(solution)/shard_map/pallas_call | solution.py:555
  251.7 7.1 %shard_map.248 = (bf16[768,3072]{1,0:T(8,128)(2,1)S(1)}, bf16[96,2048]{1,0:T(8,128)(2,1)S(1)}, bf16[96,2048]{1,0:T(8,128)(2,1)S(1)}, bf16[96,2048]{1,0:T(8,128)(2,1)S(1)}, bf16[96,2048]{1,0:T(8,128)(2,1)S(1)}) custom-call(s32[8]{0:T(128)S(1)} %concatenate.57.info_ref.refs_0_.place_ref, ...), custom_call_target="tpu_custom_call", output_to_operand_aliasing={{0}: (13, {})} | custom-call | flops 4831838208 | bytes 15728640 | tf_op jit(solution)/shard_map/pallas_call | solution.py:555
  261.2 7.2 %shard_map.249 = (bf16[768,3072]{1,0:T(8,128)(2,1)S(1)}, bf16[96,2048]{1,0:T(8,128)(2,1)S(1)}, bf16[96,2048]{1,0:T(8,128)(2,1)S(1)}, bf16[96,2048]{1,0:T(8,128)(2,1)S(1)}, bf16[96,2048]{1,0:T(8,128)(2,1)S(1)}) custom-call(s32[8]{0:T(128)S(1)} %concatenate.57.info_ref.refs_0_.place_ref, ...), custom_call_target="tpu_custom_call", output_to_operand_aliasing={{0}: (13, {})} | custom-call | flops 4831838208 | bytes 15728640 | tf_op jit(solution)/shard_map/pallas_call | solution.py:555
  268.9 7.1 %shard_map.250 = (bf16[768,3072]{1,0:T(8,128)(2,1)S(1)}, bf16[96,2048]{1,0:T(8,128)(2,1)S(1)}, bf16[96,2048]{1,0:T(8,128)(2,1)S(1)}, bf16[96,2048]{1,0:T(8,128)(2,1)S(1)}, bf16[96,2048]{1,0:T(8,128)(2,1)S(1)}) custom-call(s32[8]{0:T(128)S(1)} %concatenate.57.info_ref.refs_0_.place_ref, ...), custom_call_target="tpu_custom_call", output_to_operand_aliasing={{0}: (13, {})} | custom-call | flops 4831838208 | bytes 15728640 | tf_op jit(solution)/shard_map/pallas_call | solution.py:555
  282.8 5.7 %collective-permute-done.53 = bf16[96,2048]{1,0:T(8,128)(2,1)S(1)} collective-permute-done((bf16[96,2048]{1,0:T(8,128)(2,1)S(1)}, bf16[96,2048]{1,0:T(8,128)(2,1)S(1)}, u32[]{:S(2)}, u32[]{:S(2)}) %collective-permute-start.53) | collective-permute-done | bytes 393248 | tf_op jit(solution)/shard_map/ppermute | solution.py:57
  307.9 6.1 %collective-permute-done.55.gm_ref = bf16[96,2048]{1,0:T(8,128)(2,1)S(1)} collective-permute-done((bf16[96,2048]{1,0:T(8,128)(2,1)S(1)}, bf16[96,2048]{1,0:T(8,128)(2,1)S(1)}, u32[]{:S(2)}, u32[]{:S(2)}) %collective-permute-start.55) | collective-permute-done | bytes 393248 | tf_op jit(solution)/shard_map/ppermute | solution.py:57
  329.4 8.5 %shard_map.252 = (bf16[192,256]{1,0:T(8,128)(2,1)S(1)}, f32[64,192]{1,0:T(8,128)S(1)}, f32[16,192,128]{2,1,0:T(8,128)S(1)}) custom-call(s32[8]{0:T(128)S(1)} %concatenate.57.info_ref.refs_0_.place_ref, bf16[96,2048]{1,0:T(8,128)(2,1)S(1)} %collective-permute-done.55.gm_ref, ...), custom_call_target="tpu_custom_call", output_to_operand_aliasing={{2}: (15, {})} | custom-call | flops 3019898880 | bytes 6291456 | tf_op jit(solution)/shard_map/pallas_call | solution.py:555
  346.6 6.9 %shard_map.253 = (bf16[192,256]{1,0:T(8,128)(2,1)S(1)}, f32[64,192]{1,0:T(8,128)S(1)}, f32[16,192,128]{2,1,0:T(8,128)S(1)}) custom-call(s32[8]{0:T(128)S(1)} %concatenate.57.info_ref.refs_0_.place_ref, bf16[96,2048]{1,0:T(8,128)(2,1)S(1)} %collective-permute-done.58.gm_ref, ...), custom_call_target="tpu_custom_call", output_to_operand_aliasing={{2}: (15, {})} | custom-call | flops 3019898880 | bytes 6291456 | tf_op jit(solution)/shard_map/pallas_call | solution.py:555
  356.0 6.6 %collective-permute-done.71 = bf16[512,1024]{1,0:T(8,128)(2,1)S(1)} collective-permute-done((bf16[512,1024]{1,0:T(8,128)(2,1)S(1)}, bf16[512,1024]{1,0:T(8,128)(2,1)S(1)}, u32[]{:S(2)}, u32[]{:S(2)}) %collective-permute-start.71) | collective-permute-done | bytes 1048608 | tf_op jit(solution)/shard_map/ppermute | solution.py:66
  369.8 5.7 %collective-permute-done.74.refs_1_ = bf16[128,1024]{1,0:T(8,128)(2,1)S(1)} collective-permute-done((bf16[128,1024]{1,0:T(8,128)(2,1)S(1)}, bf16[128,1024]{1,0:T(8,128)(2,1)S(1)}, u32[]{:S(2)}, u32[]{:S(2)}) %collective-permute-start.74) | collective-permute-done | bytes 262176 | tf_op jit(solution)/shard_map/ppermute | solution.py:57
  375.5 5.5 %collective-permute-done.78.refs_2_ = bf16[128,1024]{1,0:T(8,128)(2,1)S(1)} collective-permute-done((bf16[128,1024]{1,0:T(8,128)(2,1)S(1)}, bf16[128,1024]{1,0:T(8,128)(2,1)S(1)}, u32[]{:S(2)}, u32[]{:S(2)}) %collective-permute-start.78) | collective-permute-done | bytes 262176 | tf_op jit(solution)/shard_map/ppermute | solution.py:57
  389.8 5.3 %shard_map.254 = (bf16[192,256]{1,0:T(8,128)(2,1)S(1)}, f32[64,192]{1,0:T(8,128)S(1)}, f32[16,192,128]{2,1,0:T(8,128)S(1)}) custom-call(s32[8]{0:T(128)S(1)} %concatenate.57.info_ref.refs_0_.place_ref, bf16[96,2048]{1,0:T(8,128)(2,1)S(1)} %collective-permute-done.61.gm_ref, ...), custom_call_target="tpu_custom_call", output_to_operand_aliasing={{2}: (15, {})} | custom-call | flops 3019898880 | bytes 6291456 | tf_op jit(solution)/shard_map/pallas_call | solution.py:555
  395.5 5.0 collective-permute-done.76
  401.1 9.0 %collective-permute-done.80.refs_2_ = bf16[128,1024]{1,0:T(8,128)(2,1)S(1)} collective-permute-done((bf16[128,1024]{1,0:T(8,128)(2,1)S(1)}, bf16[128,1024]{1,0:T(8,128)(2,1)S(1)}, u32[]{:S(2)}, u32[]{:S(2)}) %collective-permute-start.80) | collective-permute-done | bytes 262176 | tf_op jit(solution)/shard_map/ppermute | solution.py:57
  414.9 6.8 %collective-permute-done.81 = bf16[96,2048]{1,0:T(8,128)(2,1)S(1)} collective-permute-done((bf16[96,2048]{1,0:T(8,128)(2,1)S(1)}, bf16[96,2048]{1,0:T(8,128)(2,1)S(1)}, u32[]{:S(2)}, u32[]{:S(2)}) %collective-permute-start.81) | collective-permute-done | bytes 393248 | tf_op jit(solution)/shard_map/ppermute | solution.py:57
  436.3 5.0 collective-permute-done.88
  461.8 6.4 %collective-permute-done.94 = bf16[96,2048]{1,0:T(8,128)(2,1)S(1)} collective-permute-done((bf16[96,2048]{1,0:T(8,128)(2,1)S(1)}, bf16[96,2048]{1,0:T(8,128)(2,1)S(1)}, u32[]{:S(2)}, u32[]{:S(2)}) %collective-permute-start.94) | collective-permute-done | bytes 393248 | tf_op jit(solution)/shard_map/ppermute | solution.py:57
  (565 shorter events, 296.9 us)
Async XLA Ops:
  5.7 24.8 %collective-permute-start.3 = (bf16[96,2048]{1,0:T(8,128)(2,1)S(1)}, bf16[96,2048]{1,0:T(8,128)(2,1)}, u32[]{:S(2)}, u32[]{:S(2)}) collective-permute-start(bf16[96,2048]{1,0:T(8,128)(2,1)S(1)} %get-tuple-element.411.mine_ref), channel_id=1, source_target_pairs={{0,8},{8,16},{16,24},{24,0},{1,9},{9,17},{17,25},{25,1},{2,10},{10... | collective-permute-start | bytes 1179656 | tf_op jit(solution)/shard_map/ppermute | solution.py:57
  30.7 16.6 %collective-permute-start.4 = (bf16[512,640]{1,0:T(8,128)(2,1)S(1)}, bf16[512,640]{1,0:T(8,128)(2,1)S(1)}, u32[]{:S(2)}, u32[]{:S(2)}) collective-permute-start(bf16[512,640]{1,0:T(8,128)(2,1)S(1)} %bitcast.202), channel_id=1, source_target_pairs={{0,4},{4,0},{1,5},{5,1},{2,6},{6,2},{3,7},{7,3},{8,12},{12,8},{9,1... | collective-permute-start | bytes 1966088 | tf_op jit(solution)/shard_map/ppermute | solution.py:66
  33.5 32.0 %collective-permute-start.5 = (bf16[512,640]{1,0:T(8,128)(2,1)S(1)}, bf16[512,640]{1,0:T(8,128)(2,1)S(1)}, u32[]{:S(2)}, u32[]{:S(2)}) collective-permute-start(bf16[512,640]{1,0:T(8,128)(2,1)S(1)} %bitcast.203), channel_id=1, source_target_pairs={{0,2},{2,0},{1,3},{3,1},{4,6},{6,4},{5,7},{7,5},{8,10},{10,8},{9,1... | collective-permute-start | bytes 1966088 | tf_op jit(solution)/shard_map/ppermute | solution.py:66
  47.3 18.2 %collective-permute-start.6 = (bf16[512,640]{1,0:T(8,128)(2,1)S(1)}, bf16[512,640]{1,0:T(8,128)(2,1)S(1)}, u32[]{:S(2)}, u32[]{:S(2)}) collective-permute-start(bf16[512,640]{1,0:T(8,128)(2,1)S(1)} %collective-permute-done.4.w1.refs_4_), channel_id=1, source_target_pairs={{0,2},{2,0},{1,3},{3,1},{4,6},{6,4},{5,7},{7,5},{8,10},{10,8},{9,1... | collective-permute-start | bytes 1966088 | tf_op jit(solution)/shard_map/ppermute | solution.py:66
  54.7 21.1 %collective-permute-start.12 = (bf16[128,2048]{1,0:T(8,128)(2,1)S(1)}, bf16[128,2048]{1,0:T(8,128)(2,1)S(1)}, u32[]{:S(2)}, u32[]{:S(2)}) collective-permute-start(bf16[128,2048]{1,0:T(8,128)(2,1)S(1)} %get-tuple-element.244), channel_id=1, source_target_pairs={{0,8},{8,16},{16,24},{24,0},{1,9},{9,17},{17,25},{25,1},{2,10},{10... | collective-permute-start | bytes 1572872 | tf_op jit(solution)/shard_map/ppermute | solution.py:57
  65.0 20.2 %collective-permute-start.22 = (bf16[128,2048]{1,0:T(8,128)(2,1)}, bf16[128,2048]{1,0:T(8,128)(2,1)}, u32[]{:S(2)}, u32[]{:S(2)}) collective-permute-start(bf16[128,2048]{1,0:T(8,128)(2,1)} %get-tuple-element.269), channel_id=1, source_target_pairs={{0,24},{8,0},{16,8},{24,16},{1,25},{9,1},{17,9},{25,17},{2,26},{10... | collective-permute-start | bytes 1572872 | tf_op jit(solution)/shard_map/ppermute | solution.py:57
  85.2 16.3 %collective-permute-start.23 = (bf16[128,2048]{1,0:T(8,128)(2,1)}, bf16[128,2048]{1,0:T(8,128)(2,1)S(1)}, u32[]{:S(2)}, u32[]{:S(2)}) collective-permute-start(bf16[128,2048]{1,0:T(8,128)(2,1)} %get-tuple-element.270), channel_id=1, source_target_pairs={{0,8},{8,16},{16,24},{24,0},{1,9},{9,17},{17,25},{25,1},{2,10},{10... | collective-permute-start | bytes 1572872 | tf_op jit(solution)/shard_map/ppermute | solution.py:57
  101.5 16.6 %collective-permute-start.24 = (bf16[128,2048]{1,0:T(8,128)(2,1)S(1)}, bf16[128,2048]{1,0:T(8,128)(2,1)S(1)}, u32[]{:S(2)}, u32[]{:S(2)}) collective-permute-start(bf16[128,2048]{1,0:T(8,128)(2,1)S(1)} %collective-permute-done.23), channel_id=1, source_target_pairs={{0,8},{8,16},{16,24},{24,0},{1,9},{9,17},{17,25},{25,1},{2,10},{10... | collective-permute-start | bytes 1572872 | tf_op jit(solution)/shard_map/ppermute | solution.py:57
  106.0 20.6 %collective-permute-start.17 = (bf16[96,2048]{1,0:T(8,128)(2,1)S(1)}, bf16[96,2048]{1,0:T(8,128)(2,1)S(1)}, u32[]{:S(2)}, u32[]{:S(2)}) collective-permute-start(bf16[96,2048]{1,0:T(8,128)(2,1)S(1)} %add_convert_fusion.19), channel_id=1, source_target_pairs={{0,8},{8,16},{16,24},{24,0},{1,9},{9,17},{17,25},{25,1},{2,10},{10... | collective-permute-start | bytes 1179656 | tf_op jit(solution)/shard_map/ppermute | solution.py:57
  107.0 19.6 %collective-permute-start.16 = (bf16[96,2048]{1,0:T(8,128)(2,1)S(1)}, bf16[96,2048]{1,0:T(8,128)(2,1)S(1)}, u32[]{:S(2)}, u32[]{:S(2)}) collective-permute-start(bf16[96,2048]{1,0:T(8,128)(2,1)S(1)} %get-tuple-element.251), channel_id=1, source_target_pairs={{0,1},{1,0},{2,3},{3,2},{4,5},{5,4},{6,7},{7,6},{8,9},{9,8},{10,11... | collective-permute-start | bytes 1179656 | tf_op jit(solution)/shard_map/ppermute | solution.py:66
  118.2 35.3 %collective-permute-start.25 = (bf16[128,1024]{1,0:T(8,128)(2,1)S(1)}, bf16[128,1024]{1,0:T(8,128)(2,1)S(1)}, u32[]{:S(2)}, u32[]{:S(2)}) collective-permute-start(bf16[128,1024]{1,0:T(8,128)(2,1)S(1)} %get-tuple-element.271), channel_id=1, source_target_pairs={{0,8},{8,16},{16,24},{24,0},{1,9},{9,17},{17,25},{25,1},{2,10},{10... | collective-permute-start | bytes 786440 | tf_op jit(solution)/shard_map/ppermute | solution.py:57
  142.2 59.0 %collective-permute-start.38 = (bf16[512,2048]{1,0:T(8,128)(2,1)S(1)}, bf16[512,2048]{1,0:T(8,128)(2,1)S(1)}, u32[]{:S(2)}, u32[]{:S(2)}) collective-permute-start(bf16[512,2048]{1,0:T(8,128)(2,1)S(1)} %bitcast.220), channel_id=1, source_target_pairs={{0,4},{4,0},{1,5},{5,1},{2,6},{6,2},{3,7},{7,3},{8,12},{12,8},{9,1... | collective-permute-start | bytes 6291464 | tf_op jit(solution)/shard_map/ppermute | solution.py:66
  151.7 17.7 %collective-permute-start.27 = (bf16[128,1024]{1,0:T(8,128)(2,1)S(1)}, bf16[128,1024]{1,0:T(8,128)(2,1)S(1)}, u32[]{:S(2)}, u32[]{:S(2)}) collective-permute-start(bf16[128,1024]{1,0:T(8,128)(2,1)S(1)} %get-tuple-element.273), channel_id=1, source_target_pairs={{0,24},{8,0},{16,8},{24,16},{1,25},{9,1},{17,9},{25,17},{2,26},{10... | collective-permute-start | bytes 786440 | tf_op jit(solution)/shard_map/ppermute | solution.py:57
  153.9 26.4 %collective-permute-start.32 = (bf16[96,2048]{1,0:T(8,128)(2,1)S(1)}, bf16[96,2048]{1,0:T(8,128)(2,1)S(1)}, u32[]{:S(2)}, u32[]{:S(2)}) collective-permute-start(bf16[96,2048]{1,0:T(8,128)(2,1)S(1)} %multiply_convert_fusion.hm_ref), channel_id=1, source_target_pairs={{0,1},{1,0},{2,3},{3,2},{4,5},{5,4},{6,7},{7,6},{8,9},{9,8},{10,11... | collective-permute-start | bytes 1179656 | tf_op jit(solution)/shard_map/ppermute | solution.py:66
  169.3 73.4 %collective-permute-start.39 = (bf16[512,2048]{1,0:T(8,128)(2,1)S(1)}, bf16[512,2048]{1,0:T(8,128)(2,1)S(1)}, u32[]{:S(2)}, u32[]{:S(2)}) collective-permute-start(bf16[512,2048]{1,0:T(8,128)(2,1)S(1)} %bitcast.221), channel_id=1, source_target_pairs={{0,2},{2,0},{1,3},{3,1},{4,6},{6,4},{5,7},{7,5},{8,10},{10,8},{9,1... | collective-permute-start | bytes 6291464 | tf_op jit(solution)/shard_map/ppermute | solution.py:66
  181.9 17.8 %collective-permute-start.31 = (bf16[96,2048]{1,0:T(8,128)(2,1)S(1)}, bf16[96,2048]{1,0:T(8,128)(2,1)S(1)}, u32[]{:S(2)}, u32[]{:S(2)}) collective-permute-start(bf16[96,2048]{1,0:T(8,128)(2,1)S(1)} %get-tuple-element.278.cm_ref), channel_id=1, source_target_pairs={{0,8},{8,16},{16,24},{24,0},{1,9},{9,17},{17,25},{25,1},{2,10},{10... | collective-permute-start | bytes 1179656 | tf_op jit(solution)/shard_map/ppermute | solution.py:57
  201.2 29.7 %collective-permute-start.41 = (bf16[512,1024]{1,0:T(8,128)(2,1)S(1)}, bf16[512,1024]{1,0:T(8,128)(2,1)S(1)}, u32[]{:S(2)}, u32[]{:S(2)}) collective-permute-start(bf16[512,1024]{1,0:T(8,128)(2,1)S(1)} %bitcast.226), channel_id=1, source_target_pairs={{0,4},{4,0},{1,5},{5,1},{2,6},{6,2},{3,7},{7,3},{8,12},{12,8},{9,1... | collective-permute-start | bytes 3145736 | tf_op jit(solution)/shard_map/ppermute | solution.py:66
  204.5 38.3 %collective-permute-start.40 = (bf16[512,2048]{1,0:T(8,128)(2,1)S(1)}, bf16[512,2048]{1,0:T(8,128)(2,1)S(1)}, u32[]{:S(2)}, u32[]{:S(2)}) collective-permute-start(bf16[512,2048]{1,0:T(8,128)(2,1)S(1)} %collective-permute-done.38.p1), channel_id=1, source_target_pairs={{0,2},{2,0},{1,3},{3,1},{4,6},{6,4},{5,7},{7,5},{8,10},{10,8},{9,1... | collective-permute-start | bytes 6291464 | tf_op jit(solution)/shard_map/ppermute | solution.py:66
  281.7 19.3 %collective-permute-start.60 = (bf16[512,1024]{1,0:T(8,128)(2,1)S(1)}, bf16[512,1024]{1,0:T(8,128)(2,1)S(1)}, u32[]{:S(2)}, u32[]{:S(2)}) collective-permute-start(bf16[512,1024]{1,0:T(8,128)(2,1)S(1)} %convolution_convert_fusion.2), channel_id=1, source_target_pairs={{0,2},{2,0},{1,3},{3,1},{4,6},{6,4},{5,7},{7,5},{8,10},{10,8},{9,1... | collective-permute-start | bytes 3145736 | tf_op jit(solution)/shard_map/ppermute | solution.py:66
  298.3 24.1 %collective-permute-start.59 = (bf16[512,1024]{1,0:T(8,128)(2,1)S(1)}, bf16[512,1024]{1,0:T(8,128)(2,1)S(1)}, u32[]{:S(2)}, u32[]{:S(2)}) collective-permute-start(bf16[512,1024]{1,0:T(8,128)(2,1)S(1)} %convolution_convert_fusion.3), channel_id=1, source_target_pairs={{0,2},{2,0},{1,3},{3,1},{4,6},{6,4},{5,7},{7,5},{8,10},{10,8},{9,1... | collective-permute-start | bytes 3145736 | tf_op jit(solution)/shard_map/ppermute | solution.py:66
  306.7 104.3 %collective-permute-start.108 = (bf16[512,1024]{1,0:T(8,128)(2,1)S(1)}, bf16[512,1024]{1,0:T(8,128)(2,1)S(1)}, u32[]{:S(2)}, u32[]{:S(2)}) collective-permute-start(bf16[512,1024]{1,0:T(8,128)(2,1)S(1)} %convolution_convert_fusion), channel_id=1, source_target_pairs={{0,2},{2,0},{1,3},{3,1},{4,6},{6,4},{5,7},{7,5},{8,10},{10,8},{9,1... | collective-permute-start | bytes 3145736 | tf_op jit(solution)/shard_map/ppermute | solution.py:66
  307.8 32.6 %collective-permute-start.70 = (bf16[512,1024]{1,0:T(8,128)(2,1)S(1)}, bf16[512,1024]{1,0:T(8,128)(2,1)S(1)}, u32[]{:S(2)}, u32[]{:S(2)}) collective-permute-start(bf16[512,1024]{1,0:T(8,128)(2,1)S(1)} %add_convert_fusion.4), channel_id=1, source_target_pairs={{0,4},{4,0},{1,5},{5,1},{2,6},{6,2},{3,7},{7,3},{8,12},{12,8},{9,1... | collective-permute-start | bytes 3145736 | tf_op jit(solution)/shard_map/ppermute | solution.py:66
  340.4 22.2 %collective-permute-start.71 = (bf16[512,1024]{1,0:T(8,128)(2,1)S(1)}, bf16[512,1024]{1,0:T(8,128)(2,1)S(1)}, u32[]{:S(2)}, u32[]{:S(2)}) collective-permute-start(bf16[512,1024]{1,0:T(8,128)(2,1)S(1)} %add_convert_fusion.5), channel_id=1, source_target_pairs={{0,4},{4,0},{1,5},{5,1},{2,6},{6,2},{3,7},{7,3},{8,12},{12,8},{9,1... | collective-permute-start | bytes 3145736 | tf_op jit(solution)/shard_map/ppermute | solution.py:66
  342.7 22.2 %collective-permute-start.77 = (bf16[128,1024]{1,0:T(8,128)(2,1)S(1)}, bf16[128,1024]{1,0:T(8,128)(2,1)S(1)}, u32[]{:S(2)}, u32[]{:S(2)}) collective-permute-start(bf16[128,1024]{1,0:T(8,128)(2,1)S(1)} %get-tuple-element.341), channel_id=1, source_target_pairs={{0,24},{8,0},{16,8},{24,16},{1,25},{9,1},{17,9},{25,17},{2,26},{10... | collective-permute-start | bytes 786440 | tf_op jit(solution)/shard_map/ppermute | solution.py:57
  369.1 41.0 %collective-permute-start.84 = (bf16[512,1024]{1,0:T(8,128)(2,1)S(1)}, bf16[512,1024]{1,0:T(8,128)(2,1)S(1)}, u32[]{:S(2)}, u32[]{:S(2)}) collective-permute-start(bf16[512,1024]{1,0:T(8,128)(2,1)S(1)} %add_convert_fusion.1), channel_id=1, source_target_pairs={{0,4},{4,0},{1,5},{5,1},{2,6},{6,2},{3,7},{7,3},{8,12},{12,8},{9,1... | collective-permute-start | bytes 3145736 | tf_op jit(solution)/shard_map/ppermute | solution.py:66
  395.3 60.5 %collective-permute-start.116 = (bf16[512,256]{1,0:T(8,128)(2,1)S(1)}, bf16[512,256]{1,0:T(8,128)(2,1)S(1)}, u32[]{:S(2)}, u32[]{:S(2)}) collective-permute-start(bf16[512,256]{1,0:T(8,128)(2,1)S(1)} %convolution_convert_fusion.8), channel_id=1, source_target_pairs={{0,2},{2,0},{1,3},{3,1},{4,6},{6,4},{5,7},{7,5},{8,10},{10,8},{9,1... | collective-permute-start | bytes 786440 | tf_op jit(solution)/shard_map/ppermute | solution.py:66
  395.4 28.1 %collective-permute-start.69 = (bf16[96,2048]{1,0:T(8,128)(2,1)S(1)}, bf16[96,2048]{1,0:T(8,128)(2,1)S(1)}, u32[]{:S(2)}, u32[]{:S(2)}) collective-permute-start(bf16[96,2048]{1,0:T(8,128)(2,1)S(1)} %get-tuple-element.330), channel_id=1, source_target_pairs={{0,1},{1,0},{2,3},{3,2},{4,5},{5,4},{6,7},{7,6},{8,9},{9,8},{10,11... | collective-permute-start | bytes 1179656 | tf_op jit(solution)/shard_map/ppermute | solution.py:66
  421.9 23.4 %collective-permute-start.82 = (bf16[96,2048]{1,0:T(8,128)(2,1)S(1)}, bf16[96,2048]{1,0:T(8,128)(2,1)S(1)}, u32[]{:S(2)}, u32[]{:S(2)}) collective-permute-start(bf16[96,2048]{1,0:T(8,128)(2,1)S(1)} %add_convert_fusion.11), channel_id=1, source_target_pairs={{0,8},{8,16},{16,24},{24,0},{1,9},{9,17},{17,25},{25,1},{2,10},{10... | collective-permute-start | bytes 1179656 | tf_op jit(solution)/shard_map/ppermute | solution.py:57
  471.1 20.6 %collective-permute-start.110 = (bf16[128,1024]{1,0:T(8,128)(2,1)}, bf16[128,1024]{1,0:T(8,128)(2,1)}, u32[]{:S(2)}, u32[]{:S(2)}) collective-permute-start(bf16[128,1024]{1,0:T(8,128)(2,1)} %get-tuple-element.423), channel_id=1, source_target_pairs={{0,8},{8,16},{16,24},{24,0},{1,9},{9,17},{17,25},{25,1},{2,10},{10... | collective-permute-start | bytes 786440 | tf_op jit(solution)/shard_map/ppermute | solution.py:57
  474.7 18.2 %collective-permute-start.111 = (bf16[128,1024]{1,0:T(8,128)(2,1)S(1)}, bf16[128,1024]{1,0:T(8,128)(2,1)}, u32[]{:S(2)}, u32[]{:S(2)}) collective-permute-start(bf16[128,1024]{1,0:T(8,128)(2,1)S(1)} %copy-done.67), channel_id=1, source_target_pairs={{0,24},{8,0},{16,8},{24,16},{1,25},{9,1},{17,9},{25,17},{2,26},{10... | collective-permute-start | bytes 786440 | tf_op jit(solution)/shard_map/ppermute | solution.py:57
  491.7 18.0 %collective-permute-start.91 = (bf16[96,2048]{1,0:T(8,128)(2,1)S(1)}, bf16[96,2048]{1,0:T(8,128)(2,1)S(1)}, u32[]{:S(2)}, u32[]{:S(2)}) collective-permute-start(bf16[96,2048]{1,0:T(8,128)(2,1)S(1)} %add_convert_fusion.10.own_ref), channel_id=1, source_target_pairs={{0,1},{1,0},{2,3},{3,2},{4,5},{5,4},{6,7},{7,6},{8,9},{9,8},{10,11... | collective-permute-start | bytes 1179656 | tf_op jit(solution)/shard_map/ppermute | solution.py:66
  502.5 16.7 %collective-permute-start.113 = (bf16[128,384]{1,0:T(8,128)(2,1)S(1)}, bf16[128,384]{1,0:T(8,128)(2,1)S(1)}, u32[]{:S(2)}, u32[]{:S(2)}) collective-permute-start(bf16[128,384]{1,0:T(8,128)(2,1)S(1)} %copy-done.77), channel_id=1, source_target_pairs={{0,8},{8,16},{16,24},{24,0},{1,9},{9,17},{17,25},{25,1},{2,10},{10... | collective-permute-start | bytes 294920 | tf_op jit(solution)/shard_map/ppermute | solution.py:57
  (174 other events, 2163.8 us)
